TPU v7x, 32 devices: a whole 2x2x4 slice. The times are simulated.
32 devices in a mesh: groups: 2 (over y), depth: 16 (over z, x, core).
Axes of the slice: x: 2, y: 2, z: 4, core: 2. Of those that a mesh axis runs over, the one named last changes fastest.
Arguments:
- source: float32 [2, 2, 128, 64, 128], P('groups', None, 'depth'), parts along dimension 0, may hold values from -4 to 4
- transmit: float32 [2, 128, 64], P(None, 'depth'), may hold values from -1 to 1
- neighbours: int32 [128, 9], P('depth'), may hold values from -1 to 63, as said below
- extrapolator: float32 [128, 2, 64, 576], P('depth'), may hold values from -0.1875 to 0.1875
Outputs:
- wavefield: float32 [2, 2, 128, 64, 128], P('groups', None, 'depth'), parts along dimension 0
There are 2 independent parts, one for each index of `groups`. A program takes and returns all parts, laid end to end along the dimension named above; an argument that names none is the same for every part. Nothing has to cross between parts.
Inputs may be any that keep to these rules, and one draw needn't show every extreme that they name: `neighbours`: each row lists, in an order drawn for each tile, the tiles at strip offsets -1, 0, 1 and column offsets -1, 0, 1 of its own tile, as level-local indices strip * 8 + column, and -1 for each such tile outside the 8 x 8 tile grid.
All inputs are finite; a program needn't handle non-finite values.
Results may differ from a plain program's by a relative error of at most 0.0003.
Values sent between devices are 32-bit elements; how exact they have to be, the bound alone decides.
No kernel may reach another device: no remote copies, remote signals or barrier semaphores. Data moves between devices by JAX's collectives and lax.ppermute only.
A program may use at most 64 MiB of HBM per device.

v0:
```python
import jax
import jax.numpy as jnp
from jax import lax
from jax.sharding import PartitionSpec as P

N_LAT = 8


def from_behind(block, axis, distance):
    devices = range(lax.axis_size(axis))
    route = [(i - distance, i) for i in devices if i - distance in devices]
    return lax.ppermute(block, axis, route)


def body(source, transmit, neighbours, extrapolator):
    tiles_here = neighbours.shape[0]
    tile_len = extrapolator.shape[2]
    packets = source.shape[0]
    shots = source.shape[4]
    levels = lax.axis_size("depth") // N_LAT
    place = lax.axis_index("depth")
    strip = place // levels
    owner = levels - 1 - place % levels
    maximum_precision = lax.Precision.HIGHEST
    valid = neighbours >= 0
    local = neighbours - (strip - 1) * tiles_here
    index = jnp.where(valid, local, 0)
    keep = valid.astype(jnp.float32)[:, :, None, None]
    block_real_part = extrapolator[:, 0]
    block_imaginary_part = extrapolator[:, 1]
    upper = (owner > 0).astype(jnp.float32)
    trans_re = 1.0 + transmit[0][:, :, None]
    trans_im = transmit[1][:, :, None]

    def extrapolate(widened):
        width = widened.shape[3]
        real_green = (widened[0][index] * keep).reshape(tiles_here, 9 * tile_len, width)
        imaginary_green = (widened[1][index] * keep).reshape(tiles_here, 9 * tile_len, width)
        output_real = jnp.einsum(
            "fmg,fgh->fmh", block_real_part, real_green, precision=maximum_precision
        ) - jnp.einsum(
            "fmg,fgh->fmh", block_imaginary_part, imaginary_green, precision=maximum_precision
        )
        output_imaginary = jnp.einsum(
            "fmg,fgh->fmh", block_real_part, imaginary_green, precision=maximum_precision
        ) + jnp.einsum(
            "fmg,fgh->fmh", block_imaginary_part, real_green, precision=maximum_precision
        )
        return jnp.stack([output_real, output_imaginary], 0)

    def transmitted(field, piece):
        real_u = trans_re * field[0] - trans_im * field[1] + piece[0]
        imag_u = trans_re * field[1] + trans_im * field[0] + piece[1]
        return jnp.stack([real_u, imag_u], 0)

    width = shots // 1
    total = packets * 1
    steps = levels + total - 1

    def one_step(step, carry):
        incoming, outputs = carry
        ordinal = step - owner
        active = (ordinal >= 0) & (ordinal < total)
        piece = source[0]
        stacked = transmitted(incoming, piece)
        below = from_behind(stacked, "depth", levels)
        above = from_behind(stacked, "depth", -levels)
        result = extrapolate(jnp.concatenate([below, stacked, above], 1))
        current = outputs[0]
        chosen = jnp.where(active, result, current)
        outputs = chosen[None]
        incoming = from_behind(result, "depth", -1) * upper
        return (incoming, outputs)

    first = jnp.zeros((2, tiles_here, tile_len, width), jnp.float32)
    empty = jnp.zeros(source.shape, jnp.float32)
    final, outputs = lax.fori_loop(0, steps, one_step, (first, empty))
    return outputs


def solution(mesh):
    in_specs = (
        P("groups", None, "depth", None, None),
        P(None, "depth", None),
        P("depth", None),
        P("depth", None, None, None),
    )
    out_specs = P("groups", None, "depth", None, None)
    return jax.shard_map(body, mesh=mesh, in_specs=in_specs, out_specs=out_specs, check_vma=False)
```

profile of v0, /device:TPU:19, one launch (start us, length us, event | category | flops | bytes accessed | tf_op | source)
XLA Modules:
  0.0 111.6 jit_solution(12644641484462188556)
XLA Ops:
  0.7 3.6 %slice_bitcast_fusion.2 = (f32[8,64,576]{2,1,0:T(8,128)}, f32[8,64,576]{2,1,0:T(8,128)}) fusion(f32[8,2,64,576]{3,2,1,0:T(8,128)} %param.9), kind=kLoop, calls=%fused_computation.18 | loop fusion | bytes 4718592 | tf_op jit(solution)/shard_map/squeeze | solution.py:30
  4.3 107.3 %while.16 = (s32[]{:T(128)}, f32[2,8,64,128]{3,2,1,0:T(8,128)S(1)}, f32[1,2,8,64,128]{4,3,2,1,0:T(8,128)}, f32[8,64,1]{1,0,2:T(8,128)S(1)}, f32[8,64,1]{1,0,2:T(...) while((s32[]{:T(128)}, f32[2,8,64,128]{3,2,1,0:T(8,128)S(1)}, ...), condition=%wide.region_1.2_spmd.clone, body=%wide.region_0.1_spmd.clone.sunk | while | flops 1815872768 | bytes 79776456 | solution.py:77
  4.6 2.2 %collective-permute-start = (f32[2,8,64,128]{3,2,1,0:T(8,128)S(1)}, f32[2,8,64,128]{3,2,1,0:T(8,128)S(1)}, u32[]{:S(2)}, u32[]{:S(2)}) collective-permute-start(f32[2,8,64,128]{3,2,1,0:T(8,128)S(1)} %pad_maximum_fusion.6), channel_id=1, source_target_pairs={{2,0},{3,1},{4,2},{5,3},{6,4},{7,5},{8,6},{9,7},{10,8},{11,9},{12,... | collective-permute-start | bytes 1572872 | tf_op jit(solution)/shard_map/while/body/eval_jaxpr/ppermute | solution.py:12
  6.8 4.0 %collective-permute-start.1 = (f32[2,8,64,128]{3,2,1,0:T(8,128)S(1)}, f32[2,8,64,128]{3,2,1,0:T(8,128)S(1)}, u32[]{:S(2)}, u32[]{:S(2)}) collective-permute-start(f32[2,8,64,128]{3,2,1,0:T(8,128)S(1)} %pad_maximum_fusion.6), channel_id=1, source_target_pairs={{0,2},{1,3},{2,4},{3,5},{4,6},{5,7},{6,8},{7,9},{8,10},{9,11},{10,... | collective-permute-start | bytes 1572872 | tf_op jit(solution)/shard_map/while/body/eval_jaxpr/ppermute | solution.py:12
  11.1 17.5 %collective-permute-done = f32[2,8,64,128]{3,2,1,0:T(8,128)S(1)} collective-permute-done((f32[2,8,64,128]{3,2,1,0:T(8,128)S(1)}, f32[2,8,64,128]{3,2,1,0:T(8,128)S(1)}, u32[]{:S(2)}, u32[]{:S(2)}) %collective-permute-start) | collective-permute-done | bytes 524320 | tf_op jit(solution)/shard_map/while/body/eval_jaxpr/ppermute | solution.py:12
  28.6 3.9 %collective-permute-done.1 = f32[2,8,64,128]{3,2,1,0:T(8,128)S(1)} collective-permute-done((f32[2,8,64,128]{3,2,1,0:T(8,128)S(1)}, f32[2,8,64,128]{3,2,1,0:T(8,128)S(1)}, u32[]{:S(2)}, u32[]{:S(2)}) %collective-permute-start.1) | collective-permute-done | bytes 524320 | tf_op jit(solution)/shard_map/while/body/eval_jaxpr/ppermute | solution.py:12
  32.9 2.1 %gather_fusion.1 = f32[72,64,128]{2,1,0:T(8,128)} fusion(f32[24,64,128]{2,1,0:T(8,128)S(1)} %get-tuple-element.360, s32[1024]{0:T(1024)S(1)} %pad_clamp_fusion.2), kind=kCustom, calls=%fused_computation.1.clone.clone.1 | custom fusion | bytes 4718880 | tf_op jit(solution)/shard_map/while/body/eval_jaxpr/gather | solution.py:38
  35.0 2.1 %gather_fusion = f32[72,64,128]{2,1,0:T(8,128)} fusion(f32[24,64,128]{2,1,0:T(8,128)S(1)} %get-tuple-element.359, s32[1024]{0:T(1024)S(1)} %pad_clamp_fusion.2), kind=kCustom, calls=%fused_computation.clone.clone.1 | custom fusion | bytes 4718880 | tf_op jit(solution)/shard_map/while/body/eval_jaxpr/gather | solution.py:37
  37.1 2.3 %bitcast_multiply_fusion.3 = (f32[8,576,128]{2,1,0:T(8,128)S(1)}, f32[8,576,128]{2,1,0:T(8,128)S(1)}) fusion(f32[8,576]{1,0:T(8,128)S(1)} %mul.173, f32[8,576,128]{2,1,0:T(8,128)} %bitcast.91, f32[8,576,128]{2,1,0:T(8,128)S(1)} %bitcast.90), kind=kLoop, calls=%fused_computation.3.clone.1 | loop fusion | flops 1179648 | bytes 9455616 | tf_op jit(solution)/shard_map/while/body/eval_jaxpr/mul | solution.py:37
  39.5 1.9 %fusion.29 = f32[8,128,64]{1,2,0:T(8,128)S(1)} fusion(f32[8,576,128]{2,1,0:T(8,128)S(1)} %get-tuple-element.362, f32[8,64,576]{2,1,0:T(8,128)S(1)} %copy-done.2), kind=kOutput, calls=%fused_computation.25.clone.1 | convolution fusion | flops 452984832 | bytes 3801088 | tf_op jit(solution)/shard_map/while/body/eval_jaxpr/fmg,fgh->fmh/dot_general | solution.py:39
  41.4 1.9 %fusion.28 = f32[8,128,64]{1,2,0:T(8,128)S(1)} fusion(f32[8,576,128]{2,1,0:T(8,128)S(1)} %get-tuple-element.361, f32[8,64,576]{2,1,0:T(8,128)S(1)} %copy-done.2), kind=kOutput, calls=%fused_computation.26.clone.1 | convolution fusion | flops 452984832 | bytes 3801088 | tf_op jit(solution)/shard_map/while/body/eval_jaxpr/fmg,fgh->fmh/dot_general | solution.py:44
  47.2 2.5 %collective-permute-start.2 = (f32[2,8,64,128]{3,2,1,0:T(8,128)S(1)}, f32[2,8,64,128]{3,2,1,0:T(8,128)S(1)}, u32[]{:S(2)}, u32[]{:S(2)}) collective-permute-start(f32[2,8,64,128]{3,2,1,0:T(8,128)S(1)} %pad_maximum_fusion.8), channel_id=1, source_target_pairs={{1,0},{2,1},{3,2},{4,3},{5,4},{6,5},{7,6},{8,7},{9,8},{10,9},{11,1... | collective-permute-start | bytes 1572872 | tf_op jit(solution)/shard_map/while/body/eval_jaxpr/ppermute | solution.py:12
  50.0 8.8 %collective-permute-done.2 = f32[2,8,64,128]{3,2,1,0:T(8,128)S(1)} collective-permute-done((f32[2,8,64,128]{3,2,1,0:T(8,128)S(1)}, f32[2,8,64,128]{3,2,1,0:T(8,128)S(1)}, u32[]{:S(2)}, u32[]{:S(2)}) %collective-permute-start.2) | collective-permute-done | bytes 524320 | tf_op jit(solution)/shard_map/while/body/eval_jaxpr/ppermute | solution.py:12
  59.2 1.9 %collective-permute-start = (f32[2,8,64,128]{3,2,1,0:T(8,128)S(1)}, f32[2,8,64,128]{3,2,1,0:T(8,128)S(1)}, u32[]{:S(2)}, u32[]{:S(2)}) collective-permute-start(f32[2,8,64,128]{3,2,1,0:T(8,128)S(1)} %pad_maximum_fusion.6), channel_id=1, source_target_pairs={{2,0},{3,1},{4,2},{5,3},{6,4},{7,5},{8,6},{9,7},{10,8},{11,9},{12,... | collective-permute-start | bytes 1572872 | tf_op jit(solution)/shard_map/while/body/eval_jaxpr/ppermute | solution.py:12
  61.1 4.3 %collective-permute-start.1 = (f32[2,8,64,128]{3,2,1,0:T(8,128)S(1)}, f32[2,8,64,128]{3,2,1,0:T(8,128)S(1)}, u32[]{:S(2)}, u32[]{:S(2)}) collective-permute-start(f32[2,8,64,128]{3,2,1,0:T(8,128)S(1)} %pad_maximum_fusion.6), channel_id=1, source_target_pairs={{0,2},{1,3},{2,4},{3,5},{4,6},{5,7},{6,8},{7,9},{8,10},{9,11},{10,... | collective-permute-start | bytes 1572872 | tf_op jit(solution)/shard_map/while/body/eval_jaxpr/ppermute | solution.py:12
  65.6 17.8 %collective-permute-done = f32[2,8,64,128]{3,2,1,0:T(8,128)S(1)} collective-permute-done((f32[2,8,64,128]{3,2,1,0:T(8,128)S(1)}, f32[2,8,64,128]{3,2,1,0:T(8,128)S(1)}, u32[]{:S(2)}, u32[]{:S(2)}) %collective-permute-start) | collective-permute-done | bytes 524320 | tf_op jit(solution)/shard_map/while/body/eval_jaxpr/ppermute | solution.py:12
  85.6 2.1 %gather_fusion.1 = f32[72,64,128]{2,1,0:T(8,128)} fusion(f32[24,64,128]{2,1,0:T(8,128)S(1)} %get-tuple-element.360, s32[1024]{0:T(1024)S(1)} %pad_clamp_fusion.2), kind=kCustom, calls=%fused_computation.1.clone.clone.1 | custom fusion | bytes 4718880 | tf_op jit(solution)/shard_map/while/body/eval_jaxpr/gather | solution.py:38
  87.7 2.1 %gather_fusion = f32[72,64,128]{2,1,0:T(8,128)} fusion(f32[24,64,128]{2,1,0:T(8,128)S(1)} %get-tuple-element.359, s32[1024]{0:T(1024)S(1)} %pad_clamp_fusion.2), kind=kCustom, calls=%fused_computation.clone.clone.1 | custom fusion | bytes 4718880 | tf_op jit(solution)/shard_map/while/body/eval_jaxpr/gather | solution.py:37
  89.9 2.3 %bitcast_multiply_fusion.3 = (f32[8,576,128]{2,1,0:T(8,128)S(1)}, f32[8,576,128]{2,1,0:T(8,128)S(1)}) fusion(f32[8,576]{1,0:T(8,128)S(1)} %mul.173, f32[8,576,128]{2,1,0:T(8,128)} %bitcast.91, f32[8,576,128]{2,1,0:T(8,128)S(1)} %bitcast.90), kind=kLoop, calls=%fused_computation.3.clone.1 | loop fusion | flops 1179648 | bytes 9455616 | tf_op jit(solution)/shard_map/while/body/eval_jaxpr/mul | solution.py:37
  92.2 1.9 %fusion.29 = f32[8,128,64]{1,2,0:T(8,128)S(1)} fusion(f32[8,576,128]{2,1,0:T(8,128)S(1)} %get-tuple-element.362, f32[8,64,576]{2,1,0:T(8,128)S(1)} %copy-done.2), kind=kOutput, calls=%fused_computation.25.clone.1 | convolution fusion | flops 452984832 | bytes 3801088 | tf_op jit(solution)/shard_map/while/body/eval_jaxpr/fmg,fgh->fmh/dot_general | solution.py:39
  94.2 1.9 %fusion.28 = f32[8,128,64]{1,2,0:T(8,128)S(1)} fusion(f32[8,576,128]{2,1,0:T(8,128)S(1)} %get-tuple-element.361, f32[8,64,576]{2,1,0:T(8,128)S(1)} %copy-done.2), kind=kOutput, calls=%fused_computation.26.clone.1 | convolution fusion | flops 452984832 | bytes 3801088 | tf_op jit(solution)/shard_map/while/body/eval_jaxpr/fmg,fgh->fmh/dot_general | solution.py:44
  98.1 1.9 %convolution_add_fusion.2 = f32[8,128,64]{1,2,0:T(8,128)S(1)} fusion(f32[8,128,64]{1,2,0:T(8,128)S(1)} %fusion.28, f32[8,576,128]{2,1,0:T(8,128)S(1)} %get-tuple-element.362, f32[8,64,576]{2,1,0:T(8,128)S(1)} %copy-done.1), kind=kOutput, calls=%fused_computation.5.clone.1 | convolution fusion | flops 453050368 | bytes 4063232 | tf_op jit(solution)/shard_map/while/body/eval_jaxpr/fmg,fgh->fmh/dot_general | solution.py:46
  100.0 2.4 %collective-permute-start.2 = (f32[2,8,64,128]{3,2,1,0:T(8,128)S(1)}, f32[2,8,64,128]{3,2,1,0:T(8,128)S(1)}, u32[]{:S(2)}, u32[]{:S(2)}) collective-permute-start(f32[2,8,64,128]{3,2,1,0:T(8,128)S(1)} %pad_maximum_fusion.8), channel_id=1, source_target_pairs={{1,0},{2,1},{3,2},{4,3},{5,4},{6,5},{7,6},{8,7},{9,8},{10,9},{11,1... | collective-permute-start | bytes 1572872 | tf_op jit(solution)/shard_map/while/body/eval_jaxpr/ppermute | solution.py:12
  102.7 8.9 %collective-permute-done.2 = f32[2,8,64,128]{3,2,1,0:T(8,128)S(1)} collective-permute-done((f32[2,8,64,128]{3,2,1,0:T(8,128)S(1)}, f32[2,8,64,128]{3,2,1,0:T(8,128)S(1)}, u32[]{:S(2)}, u32[]{:S(2)}) %collective-permute-start.2) | collective-permute-done | bytes 524320 | tf_op jit(solution)/shard_map/while/body/eval_jaxpr/ppermute | solution.py:12
  (65 shorter events, 10.5 us)
Async XLA Ops:
  0.7 3.6 %copy-start.8 = (f32[2,8,64]{2,1,0:T(8,128)S(1)}, f32[2,8,64]{2,1,0:T(8,128)}, u32[]{:S(2)}) copy-start(f32[2,8,64]{2,1,0:T(8,128)} %param.7) | copy-start | bytes 12292
  0.7 3.6 %copy-start.7 = (s32[8,9]{1,0:T(8,128)S(1)}, s32[8,9]{1,0:T(8,128)}, u32[]{:S(2)}) copy-start(s32[8,9]{1,0:T(8,128)} %param.8) | copy-start | bytes 868
  0.7 3.6 %copy-start.3 = (f32[1,2,8,64,128]{4,3,2,1,0:T(8,128)S(1)}, f32[1,2,8,64,128]{4,3,2,1,0:T(8,128)}, u32[]{:S(2)}) copy-start(f32[1,2,8,64,128]{4,3,2,1,0:T(8,128)} %param.6) | copy-start | bytes 1572868
  4.6 24.0 %collective-permute-start = (f32[2,8,64,128]{3,2,1,0:T(8,128)S(1)}, f32[2,8,64,128]{3,2,1,0:T(8,128)S(1)}, u32[]{:S(2)}, u32[]{:S(2)}) collective-permute-start(f32[2,8,64,128]{3,2,1,0:T(8,128)S(1)} %pad_maximum_fusion.6), channel_id=1, source_target_pairs={{2,0},{3,1},{4,2},{5,3},{6,4},{7,5},{8,6},{9,7},{10,8},{11,9},{12,... | collective-permute-start | bytes 1572872 | tf_op jit(solution)/shard_map/while/body/eval_jaxpr/ppermute | solution.py:12
  6.8 25.7 %collective-permute-start.1 = (f32[2,8,64,128]{3,2,1,0:T(8,128)S(1)}, f32[2,8,64,128]{3,2,1,0:T(8,128)S(1)}, u32[]{:S(2)}, u32[]{:S(2)}) collective-permute-start(f32[2,8,64,128]{3,2,1,0:T(8,128)S(1)} %pad_maximum_fusion.6), channel_id=1, source_target_pairs={{0,2},{1,3},{2,4},{3,5},{4,6},{5,7},{6,8},{7,9},{8,10},{9,11},{10,... | collective-permute-start | bytes 1572872 | tf_op jit(solution)/shard_map/while/body/eval_jaxpr/ppermute | solution.py:12
  35.0 2.1 %copy-start = (f32[72,64,128]{2,1,0:T(8,128)S(1)}, f32[72,64,128]{2,1,0:T(8,128)}, u32[]{:S(2)}) copy-start(f32[72,64,128]{2,1,0:T(8,128)} %gather_fusion.1) | copy-start | bytes 7077892 | tf_op jit(solution)/shard_map/while
  37.1 2.3 %copy-start.2 = (f32[8,64,576]{2,1,0:T(8,128)S(1)}, f32[8,64,576]{2,1,0:T(8,128)}, u32[]{:S(2)}) copy-start(f32[8,64,576]{2,1,0:T(8,128)} %get-tuple-element.399) | copy-start | bytes 3538948 | tf_op jit(solution)/shard_map/while
  41.4 2.0 %copy-start.1 = (f32[8,64,576]{2,1,0:T(8,128)S(1)}, f32[8,64,576]{2,1,0:T(8,128)}, u32[]{:S(2)}) copy-start(f32[8,64,576]{2,1,0:T(8,128)} %get-tuple-element.400) | copy-start | bytes 3538948 | tf_op jit(solution)/shard_map/while
  45.3 4.5 %copy-start.5 = (f32[1,2,8,64,128]{4,3,2,1,0:T(8,128)S(1)}, f32[1,2,8,64,128]{4,3,2,1,0:T(8,128)}, u32[]{:S(2)}) copy-start(f32[1,2,8,64,128]{4,3,2,1,0:T(8,128)} %get-tuple-element.379) | copy-start | bytes 1572868 | tf_op jit(solution)/shard_map/while
  47.2 11.7 %copy-start.4 = (f32[1,2,8,64,128]{4,3,2,1,0:T(8,128)S(1)}, f32[1,2,8,64,128]{4,3,2,1,0:T(8,128)}, u32[]{:S(2)}) copy-start(f32[1,2,8,64,128]{4,3,2,1,0:T(8,128)} %get-tuple-element.419) | copy-start | bytes 1572868 | tf_op jit(solution)/shard_map/while
  47.2 11.5 %collective-permute-start.2 = (f32[2,8,64,128]{3,2,1,0:T(8,128)S(1)}, f32[2,8,64,128]{3,2,1,0:T(8,128)S(1)}, u32[]{:S(2)}, u32[]{:S(2)}) collective-permute-start(f32[2,8,64,128]{3,2,1,0:T(8,128)S(1)} %pad_maximum_fusion.8), channel_id=1, source_target_pairs={{1,0},{2,1},{3,2},{4,3},{5,4},{6,5},{7,6},{8,7},{9,8},{10,9},{11,1... | collective-permute-start | bytes 1572872 | tf_op jit(solution)/shard_map/while/body/eval_jaxpr/ppermute | solution.py:12
  50.0 8.8 %copy-start.6 = (f32[1,2,8,64,128]{4,3,2,1,0:T(8,128)}, f32[1,2,8,64,128]{4,3,2,1,0:T(8,128)S(1)}, u32[]{:S(2)}) copy-start(f32[1,2,8,64,128]{4,3,2,1,0:T(8,128)S(1)} %maximum_select_fusion.2) | copy-start | bytes 1572868 | tf_op jit(solution)/shard_map/while
  59.2 24.3 %collective-permute-start = (f32[2,8,64,128]{3,2,1,0:T(8,128)S(1)}, f32[2,8,64,128]{3,2,1,0:T(8,128)S(1)}, u32[]{:S(2)}, u32[]{:S(2)}) collective-permute-start(f32[2,8,64,128]{3,2,1,0:T(8,128)S(1)} %pad_maximum_fusion.6), channel_id=1, source_target_pairs={{2,0},{3,1},{4,2},{5,3},{6,4},{7,5},{8,6},{9,7},{10,8},{11,9},{12,... | collective-permute-start | bytes 1572872 | tf_op jit(solution)/shard_map/while/body/eval_jaxpr/ppermute | solution.py:12
  61.1 24.2 %collective-permute-start.1 = (f32[2,8,64,128]{3,2,1,0:T(8,128)S(1)}, f32[2,8,64,128]{3,2,1,0:T(8,128)S(1)}, u32[]{:S(2)}, u32[]{:S(2)}) collective-permute-start(f32[2,8,64,128]{3,2,1,0:T(8,128)S(1)} %pad_maximum_fusion.6), channel_id=1, source_target_pairs={{0,2},{1,3},{2,4},{3,5},{4,6},{5,7},{6,8},{7,9},{8,10},{9,11},{10,... | collective-permute-start | bytes 1572872 | tf_op jit(solution)/shard_map/while/body/eval_jaxpr/ppermute | solution.py:12
  87.7 2.1 %copy-start = (f32[72,64,128]{2,1,0:T(8,128)S(1)}, f32[72,64,128]{2,1,0:T(8,128)}, u32[]{:S(2)}) copy-start(f32[72,64,128]{2,1,0:T(8,128)} %gather_fusion.1) | copy-start | bytes 7077892 | tf_op jit(solution)/shard_map/while
  89.9 2.3 %copy-start.2 = (f32[8,64,576]{2,1,0:T(8,128)S(1)}, f32[8,64,576]{2,1,0:T(8,128)}, u32[]{:S(2)}) copy-start(f32[8,64,576]{2,1,0:T(8,128)} %get-tuple-element.399) | copy-start | bytes 3538948 | tf_op jit(solution)/shard_map/while
  94.2 2.0 %copy-start.1 = (f32[8,64,576]{2,1,0:T(8,128)S(1)}, f32[8,64,576]{2,1,0:T(8,128)}, u32[]{:S(2)}) copy-start(f32[8,64,576]{2,1,0:T(8,128)} %get-tuple-element.400) | copy-start | bytes 3538948 | tf_op jit(solution)/shard_map/while
  98.0 4.4 %copy-start.5 = (f32[1,2,8,64,128]{4,3,2,1,0:T(8,128)S(1)}, f32[1,2,8,64,128]{4,3,2,1,0:T(8,128)}, u32[]{:S(2)}) copy-start(f32[1,2,8,64,128]{4,3,2,1,0:T(8,128)} %get-tuple-element.379) | copy-start | bytes 1572868 | tf_op jit(solution)/shard_map/while
  100.0 11.7 %copy-start.4 = (f32[1,2,8,64,128]{4,3,2,1,0:T(8,128)S(1)}, f32[1,2,8,64,128]{4,3,2,1,0:T(8,128)}, u32[]{:S(2)}) copy-start(f32[1,2,8,64,128]{4,3,2,1,0:T(8,128)} %get-tuple-element.419) | copy-start | bytes 1572868 | tf_op jit(solution)/shard_map/while
  100.0 11.5 %collective-permute-start.2 = (f32[2,8,64,128]{3,2,1,0:T(8,128)S(1)}, f32[2,8,64,128]{3,2,1,0:T(8,128)S(1)}, u32[]{:S(2)}, u32[]{:S(2)}) collective-permute-start(f32[2,8,64,128]{3,2,1,0:T(8,128)S(1)} %pad_maximum_fusion.8), channel_id=1, source_target_pairs={{1,0},{2,1},{3,2},{4,3},{5,4},{6,5},{7,6},{8,7},{9,8},{10,9},{11,1... | collective-permute-start | bytes 1572872 | tf_op jit(solution)/shard_map/while/body/eval_jaxpr/ppermute | solution.py:12
  102.7 8.9 %copy-start.6 = (f32[1,2,8,64,128]{4,3,2,1,0:T(8,128)}, f32[1,2,8,64,128]{4,3,2,1,0:T(8,128)S(1)}, u32[]{:S(2)}) copy-start(f32[1,2,8,64,128]{4,3,2,1,0:T(8,128)S(1)} %maximum_select_fusion.2) | copy-start | bytes 1572868 | tf_op jit(solution)/shard_map/while
where the time goes:
time: 112 us
  waiting for transfers between devices  58.7 us (52%)
  starting transfers between devices  17.3 us (15%)
  matrix products  15.3 us (14%)
  local copies, waits for them, and re-layouts  13 us (12%)
  other arithmetic  6.8 us (6%)
    ppermute x6, waiting for transfers between devices, from_behind(): return lax.ppermute(block, axis, route)  58.7 us
    ppermute x6, starting transfers between devices, from_behind(): return lax.ppermute(block, axis, route)  17.3 us
    mul x2, other arithmetic, extrapolate(): widened[0][index] * keep  4.67 us
    gather x2, local copies, waits for them, and re-layouts, extrapolate(): widened[0][index] * keep  4.26 us
    gather x2, local copies, waits for them, and re-layouts, extrapolate(): widened[1][index] * keep  4.23 us
    dot_general x2, matrix products, extrapolate(): jnp.einsum('fmg,fgh->fmh', block_real_part, imaginary_green, precision=ma...  3.88 us
    dot_general x2, matrix products, extrapolate(): jnp.einsum('fmg,fgh->fmh', block_real_part, real_green, precision=maximum...  3.88 us
    dot_general x2, matrix products, extrapolate(): jnp.einsum('fmg,fgh->fmh', block_imaginary_part, real_green, precision=ma...  3.78 us
  transfers between devices with their start and end apart: 6, of which 6 were waited for; matrix products, arithmetic and copies ran while one was open for 1% of the time, Pallas kernels for 0%

commit v1 on v0

v1 whole, which is shorter than its diff:
```python
import functools

import jax
import jax.numpy as jnp
from jax import lax
from jax.experimental import pallas as pl
from jax.experimental.pallas import tpu as pltpu
from jax.sharding import PartitionSpec as P

N_LAT = 8
NEAR_PIECES = (8,)
FAR_PIECES = (8,)
VMEM = pl.BlockSpec(memory_space=pltpu.VMEM)
SMEM = pl.BlockSpec(memory_space=pltpu.SMEM)
LIMIT = 24 * 1024 * 1024


def split(value):
    high = value.astype(jnp.bfloat16)
    low = (value - high.astype(jnp.float32)).astype(jnp.bfloat16)
    return high, low


def arrange_kernel(strip_ref, neighbours_ref, block_ref, out_ref, padded, slot_of):
    tile = pl.program_id(0)
    tiles = pl.num_programs(0)
    strip = strip_ref[0]
    parity = lax.rem(strip, 2)
    points = block_ref.shape[2]
    width = 2 * points
    whole = 9 * points // width * width
    padded[:, :, :whole] = block_ref[0, :, :, :whole]
    padded[:, :, whole : 9 * points] = block_ref[0, :, :, whole:]
    for k in range(10):
        slot_of[k] = -1
    for s in range(9):
        index = neighbours_ref[tile, s]
        safe = jnp.maximum(index, 0)
        offset = lax.div(safe, tiles) - strip
        column = lax.rem(safe, tiles) - tile + 1
        group = jnp.where(offset == 0, 0, jnp.where(offset == 1 - 2 * parity, 1, 2))
        slot_of[jnp.where(index >= 0, group * 3 + column, 9)] = s
    lane = lax.broadcasted_iota(jnp.int32, (points, width), 1)
    for group in range(3):
        found = [slot_of[group * 3 + j] for j in range(3)]
        safe = [jnp.maximum(s, 0) for s in found]
        for part in range(2):
            loaded = []
            for j in range(3):
                start = pl.multiple_of(lax.div(safe[j], 2) * width, width)
                value = padded[part, :, pl.ds(start, width)]
                value = pltpu.roll(value, lax.rem(safe[j] + j, 2) * points, 1)
                loaded.append(jnp.where(found[j] >= 0, value, 0.0))
            first = jnp.where(lane < points, loaded[0], loaded[1])
            for at, value in ((0, first), (width, loaded[2][:, :points])):
                high, low = split(value)
                columns = slice(at, at + value.shape[1])
                out_ref[0, group, part * points : (part + 1) * points, columns] = high
                out_ref[0, group, (2 + part) * points : (3 + part) * points, columns] = low


def arrange(strip, neighbours, extrapolator):
    tiles, _, points, inputs = extrapolator.shape
    shape = (3, 4 * points, 3 * points)
    return pl.pallas_call(
        arrange_kernel,
        grid=(tiles,),
        in_specs=[SMEM, SMEM, pl.BlockSpec((1, 2, points, inputs), lambda t: (t, 0, 0, 0))],
        out_specs=pl.BlockSpec((1, *shape), lambda t: (t, 0, 0, 0)),
        out_shape=jax.ShapeDtypeStruct((tiles, *shape), jnp.bfloat16),
        scratch_shapes=[pltpu.VMEM((2, points, 10 * points), jnp.float32), pltpu.SMEM((10,), jnp.int32)],
        compiler_params=pltpu.CompilerParams(vmem_limit_bytes=LIMIT),
        cost_estimate=pl.CostEstimate(flops=4_000_000, bytes_accessed=6_000_000, transcendentals=0),
    )(strip, neighbours, extrapolator)


def put(field, high_ref, low_ref, at, part, shots):
    tiles, points, _ = field.shape
    high, low = split(field.reshape(tiles * points, shots))
    rows = slice((1 + at) * points, (1 + at + tiles) * points)
    columns = slice(part * shots, (part + 1) * shots)
    high_ref[rows, columns] = high
    low_ref[rows, columns] = low


def clear_ends(ref, points):
    rows = ref.shape[0]
    zero = jnp.zeros((points, ref.shape[1]), ref.dtype)
    ref[0:points] = zero
    ref[rows - points : rows] = zero


def product(blocks, high_ref, low_ref, tile, points):
    rows = slice(tile * points, (tile + 3) * points)
    first = jnp.dot(blocks, high_ref[rows], preferred_element_type=jnp.float32)
    second = jnp.dot(blocks[: 2 * points], low_ref[rows], preferred_element_type=jnp.float32)
    return first[: 2 * points] + (first[2 * points :] + second)


def complex_parts(four, points, shots):
    real = four[:points, :shots] - four[points:, shots:]
    imaginary = four[:points, shots:] + four[points:, :shots]
    return real, imaginary


def near_kernel(pieces, *refs):
    blocks_ref, source_ref, transmit_ref, incoming_ref = refs[:4]
    near_refs = refs[4 : 4 + pieces]
    out_ref, own_high, own_low, near_high, near_low = refs[4 + pieces :]
    _, tiles, points, shots = source_ref.shape
    for ref in (own_high, own_low, near_high, near_low):
        clear_ends(ref, points)
    real, imaginary = transmitted(
        source_ref[0], source_ref[1], transmit_ref[0], transmit_ref[1], incoming_ref[0], incoming_ref[1]
    )
    put(real, own_high, own_low, 0, 0, shots)
    put(imaginary, own_high, own_low, 0, 1, shots)
    at = 0
    for ref in near_refs:
        for part in range(2):
            put(ref[part], near_high, near_low, at, part, shots)
        at += ref.shape[1]
    for tile in range(tiles):
        four = product(blocks_ref[tile, 0], own_high, own_low, tile, points)
        four += product(blocks_ref[tile, 1], near_high, near_low, tile, points)
        out_ref[0, tile], out_ref[1, tile] = complex_parts(four, points, shots)


def near_sum(blocks, source, transmit, incoming, near):
    _, tiles, points, shots = source.shape
    rows = (tiles + 2) * points
    return pl.pallas_call(
        functools.partial(near_kernel, len(near)),
        in_specs=[VMEM] * (4 + len(near)),
        out_specs=VMEM,
        out_shape=jax.ShapeDtypeStruct(source.shape, jnp.float32),
        scratch_shapes=[pltpu.VMEM((rows, 2 * shots), jnp.bfloat16)] * 4,
        compiler_params=pltpu.CompilerParams(vmem_limit_bytes=LIMIT),
        cost_estimate=pl.CostEstimate(flops=1_000_000_000, bytes_accessed=5_000_000, transcendentals=0),
    )(blocks, source, transmit, incoming, *near)


def transmitted(source_real, source_imaginary, transmit_real, transmit_imaginary, real, imaginary):
    factor = 1.0 + transmit_real
    return (
        factor * real - transmit_imaginary * imaginary + source_real,
        factor * imaginary + transmit_imaginary * real + source_imaginary,
    )


def far_kernel(pieces, sent, *refs):
    active_ref, blocks_ref, partial_ref, before_ref = refs[:4]
    refs = refs[4:]
    if sent:
        source_ref, transmit_ref = refs[:2]
        refs = refs[2:]
    far_refs = refs[:pieces]
    out_ref = refs[pieces]
    sent_refs = refs[pieces + 1 : pieces + 1 + len(sent)]
    high_ref, low_ref = refs[pieces + 1 + len(sent) :]
    _, tiles, points, shots = partial_ref.shape
    clear_ends(high_ref, points)
    clear_ends(low_ref, points)
    at = 0
    for ref in far_refs:
        for part in range(2):
            put(ref[part], high_ref, low_ref, at, part, shots)
        at += ref.shape[1]
    active = active_ref[0] > 0
    where_sent = [(k, j) for k, count in enumerate(sent) for j in range(count)]
    for tile in range(tiles):
        four = product(blocks_ref[tile, 0], high_ref, low_ref, tile, points)
        real, imaginary = complex_parts(four, points, shots)
        real += partial_ref[0, tile]
        imaginary += partial_ref[1, tile]
        out_ref[0, tile] = jnp.where(active, real, before_ref[0, tile])
        out_ref[1, tile] = jnp.where(active, imaginary, before_ref[1, tile])
        if sent:
            k, j = where_sent[tile]
            sent_refs[k][0, j], sent_refs[k][1, j] = transmitted(
                source_ref[0, tile],
                source_ref[1, tile],
                transmit_ref[0, tile],
                transmit_ref[1, tile],
                real,
                imaginary,
            )


def far_sum(active, blocks, partial, before, below, far, sent):
    _, tiles, points, shots = partial.shape
    rows = (tiles + 2) * points
    far_blocks = pl.BlockSpec((tiles, 1, *blocks.shape[2:]), lambda i: (0, 2, 0, 0))
    whole = lambda a: pl.BlockSpec(a.shape, lambda i: (0,) * a.ndim)
    shapes = [jax.ShapeDtypeStruct(partial.shape, jnp.float32)]
    shapes += [jax.ShapeDtypeStruct((2, count, points, shots), jnp.float32) for count in sent]
    rest = (partial, before, *below, *far)
    return pl.pallas_call(
        functools.partial(far_kernel, len(far), sent),
        grid=(1,),
        in_specs=[SMEM, far_blocks, *map(whole, rest)],
        out_specs=tuple(map(whole, shapes)),
        out_shape=tuple(shapes),
        scratch_shapes=[pltpu.VMEM((rows, 2 * shots), jnp.bfloat16)] * 2,
        compiler_params=pltpu.CompilerParams(vmem_limit_bytes=LIMIT),
        cost_estimate=pl.CostEstimate(flops=500_000_000, bytes_accessed=4_000_000, transcendentals=0),
    )(active, blocks, *rest)


def send(value, route):
    return lax.ppermute(value, "depth", route)


def body(source, transmit, neighbours, extrapolator):
    field = source[0]
    _, tiles, points, shots = field.shape
    levels = lax.axis_size("depth") // N_LAT
    place = lax.axis_index("depth")
    strip = place // levels
    level = levels - 1 - place % levels
    strips = range(N_LAT)

    def at(s, n):
        return s * levels + levels - 1 - n

    def far_of(s):
        return s + 1 if s % 2 else s - 1

    wide = jnp.broadcast_to(transmit[..., None], field.shape)
    zero = jnp.zeros_like(field)
    u = jnp.stack(transmitted(field[0], field[1], wide[0], wide[1], zero[0], zero[1]))
    sent = (u,)
    below = ()
    if levels > 1:
        up_one = [(p, p + 1) for p in range(N_LAT * levels) if (p + 1) % levels]
        packed = jnp.concatenate([field.reshape(-1, shots), transmit.reshape(-1, shots)], 0)
        packed = send(packed, up_one)
        rows = 2 * tiles * points
        next_field = packed[:rows].reshape(field.shape)
        next_transmit = packed[rows:].reshape(transmit.shape)
        below = (next_field, jnp.broadcast_to(next_transmit[..., None], field.shape))
    blocks = arrange(strip[None], neighbours, extrapolator)
    incoming = zero
    output = zero
    for n in range(levels):
        m = max(n - 1, 0)
        near = tuple(send(piece, [(at(s, m), at(s ^ 1, n)) for s in strips]) for piece in sent)
        far = tuple(send(piece, [(at(s, m), at(far_of(s), n)) for s in strips if far_of(s) in strips]) for piece in sent)
        if n:
            incoming = send(output, [(at(s, m), at(s, n)) for s in strips])
        partial = near_sum(blocks, field, wide, incoming, near)
        last = n == levels - 1
        counts = () if last else (tiles,)
        output, *sent = far_sum(
            (level == n).astype(jnp.int32)[None], blocks, partial, output, () if last else below, far, counts
        )
    return output[None]


def solution(mesh):
    in_specs = (
        P("groups", None, "depth", None, None),
        P(None, "depth", None),
        P("depth", None),
        P("depth", None, None, None),
    )
    out_specs = P("groups", None, "depth", None, None)
    return jax.shard_map(body, mesh=mesh, in_specs=in_specs, out_specs=out_specs, check_vma=False)
```

time: 112 us -> 53.4 us (0.48)
  the two profiles are of different devices: /device:TPU:19 before, /device:TPU:24 now
where the time goes in v1:
time: 53.4 us; the launch traced here: 52.6 us
  waiting for transfers between devices  13.8 us (26%)
  Pallas kernels  13 us (24%)
  starting transfers between devices  11.1 us (21%)
  local copies, waits for them, and re-layouts  9.72 us (18%)
  other arithmetic  4.68 us (9%)
    ppermute x6, waiting for transfers between devices, send(): return lax.ppermute(value, 'depth', route)  13.8 us
    ppermute x6, starting transfers between devices, send(): return lax.ppermute(value, 'depth', route)  11.1 us
    unnamed x22, local copies, waits for them, and re-layouts  6.71 us
    pallas_call x2, Pallas kernels, far_sum(): pl.pallas_call(functools.partial(far_kernel, len(far), sent), grid=(1,),...  5.37 us
    pallas_call x2, Pallas kernels, near_sum(): pl.pallas_call(functools.partial(near_kernel, len(near)), in_specs=[VMEM]...  4.59 us
    pallas_call x1, Pallas kernels, arrange(): pl.pallas_call(arrange_kernel, grid=(tiles,), in_specs=[SMEM, SMEM, pl.Bl...  3.06 us
    concatenate x1, other arithmetic, body(): jnp.concatenate([field.reshape(-1, shots), transmit.reshape(-1, shots)], 0)  1.87 us
    add x1, other arithmetic, transmitted(): factor * real - transmit_imaginary * imaginary + source_real  1.23 us
  transfers between devices with their start and end apart: 6, of which 2 were waited for; matrix products, arithmetic and copies ran while one was open for 9% of the time, Pallas kernels for 15%

profile of v1, /device:TPU:24, one launch (start us, length us, event | category | flops | bytes accessed | tf_op | source)
XLA Modules:
  0.0 52.6 jit_solution(7489447843908266376)
XLA Ops:
  0.0 0.7 %subtract_bitcast_fusion = (f32[8,64]{1,0:T(8,128)S(1)}, f32[8,64]{1,0:T(8,128)S(1)}) fusion(f32[2,8,64]{2,1,0:T(8,128)} %param.5), kind=kLoop, calls=%fused_computation.5 | loop fusion | flops 2560 | bytes 8192 | tf_op jit(solution)/shard_map/sub | solution.py:146
  0.7 1.2 %bitcast_add_fusion.1 = (f32[1,8,64,128]{3,2,1,0:T(8,128)S(1)}, f32[1,8,64,128]{3,2,1,0:T(8,128)S(1)}) fusion(f32[1,2,8,64,128]{4,3,2,1,0:T(8,128)} %param.4, f32[8,64]{1,0:T(8,128)S(1)} %get-tuple-element.11, f32[8,64]{1,0:T(8,128)S(1)} %get-tuple-element.12), kind=kLoop, calls=%fused_computation.3 | loop fusion | flops 131072 | bytes 1052672 | tf_op jit(solution)/shard_map/add | solution.py:146
  2.0 0.9 %pad_maximum_fusion.1 = f32[2,8,64,128]{3,2,1,0:T(8,128)} fusion(f32[1,8,64,128]{3,2,1,0:T(8,128)S(1)} %get-tuple-element.10, f32[1,8,64,128]{3,2,1,0:T(8,128)S(1)} %get-tuple-element.9), kind=kLoop, calls=%fused_computation.1 | loop fusion | flops 131072 | bytes 1048576 | tf_op jit(solution)/shard_map/stack | solution.py:231
  2.8 1.4 %collective-permute-start = (f32[2,8,64,128]{3,2,1,0:T(8,128)}, f32[2,8,64,128]{3,2,1,0:T(8,128)}, u32[]{:S(2)}, u32[]{:S(2)}) collective-permute-start(f32[2,8,64,128]{3,2,1,0:T(8,128)} %pad_maximum_fusion.1), channel_id=1, source_target_pairs={{1,3},{3,1},{5,7},{7,5},{9,11},{11,9},{13,15},{15,13},{17,19},{19,... | collective-permute-start | bytes 1572872 | tf_op jit(solution)/shard_map/ppermute | solution.py:211
  4.3 0.8 %reshape.42 = f32[8,128]{1,0:T(8,128)S(1)} reshape(f32[2,8,64]{2,1,0:T(8,128)} %param.5) | data formatting | bytes 8192 | tf_op jit(solution)/shard_map/reshape | solution.py:236
  5.0 1.9 %pad_maximum_fusion = f32[1032,128]{1,0:T(8,128)} fusion(f32[8,128]{1,0:T(8,128)S(1)} %reshape.42, f32[1024,128]{1,0:T(8,128)} %bitcast.15), kind=kLoop, calls=%fused_computation | loop fusion | flops 132096 | bytes 1056768 | tf_op jit(solution)/shard_map/concatenate | solution.py:236
  6.9 4.3 %collective-permute-start.1 = (f32[1032,128]{1,0:T(8,128)}, f32[1032,128]{1,0:T(8,128)}, u32[]{:S(2)}, u32[]{:S(2)}) collective-permute-start(f32[1032,128]{1,0:T(8,128)} %pad_maximum_fusion), channel_id=1, source_target_pairs={{0,1},{2,3},{4,5},{6,7},{8,9},{10,11},{12,13},{14,15},{16,17},{18,... | collective-permute-start | bytes 1585160 | tf_op jit(solution)/shard_map/ppermute | solution.py:211
  11.2 1.5 %collective-permute-start.2 = (f32[2,8,64,128]{3,2,1,0:T(8,128)}, f32[2,8,64,128]{3,2,1,0:T(8,128)}, u32[]{:S(2)}, u32[]{:S(2)}) collective-permute-start(f32[2,8,64,128]{3,2,1,0:T(8,128)} %pad_maximum_fusion.1), channel_id=1, source_target_pairs={{3,5},{5,3},{7,9},{9,7},{11,13},{13,11},{19,21},{21,19},{23,25},{2... | collective-permute-start | bytes 1572872 | tf_op jit(solution)/shard_map/ppermute | solution.py:211
  12.7 1.7 %copy-done.6 = f32[8,2,64,576]{3,2,1,0:T(8,128)S(1)} copy-done((f32[8,2,64,576]{3,2,1,0:T(8,128)S(1)}, f32[8,2,64,576]{3,2,1,0:T(8,128)}, u32[]{:S(2)}) %copy-start.6) | copy-done | bytes 2359320
  14.4 3.1 %shard_map.46.refs_0_.refs_1_ = bf16[8,3,256,192]{3,2,1,0:T(8,128)(2,1)S(1)} custom-call(s32[1]{0:T(128)} %bitcast.1.strip_ref, s32[8,9]{1,0:T(8,128)S(1)} %copy-done.9, f32[8,2,64,576]{3,2,1,0:T(8,128)S(1)} %copy-done.6), custom_call_target="tpu_custom_call" | custom-call | flops 4000000 | bytes 6000000 | tf_op jit(solution)/shard_map/pallas_call | solution.py:65
  17.8 2.4 %shard_map.47.refs_2_ = f32[2,8,64,128]{3,2,1,0:T(8,128)S(1)} custom-call(bf16[8,3,256,192]{3,2,1,0:T(8,128)(2,1)S(1)} %shard_map.46.refs_0_.refs_1_, f32[2,8,64,128]{3,2,1,0:T(8,128)S(1)} %bitcast.16, f32[2,8,64,128]{3,2,1,0:T(8,128)S(1)} %broadcast_in_dim.39.refs_2_, f32[2,8,64,128]{3,2,1,0:T(8,128)S(1)} %broadcast_in_dim.42.refs_3_, ...), custom_call_target="tpu_custom_call" | custom-call | flops 1000000000 | bytes 5000000 | tf_op jit(solution)/shard_map/pallas_call | solution.py:132
  20.2 0.8 %copy-done.7 = f32[2,8,64,128]{3,2,1,0:T(8,128)} copy-done((f32[2,8,64,128]{3,2,1,0:T(8,128)}, f32[2,8,64,128]{3,2,1,0:T(8,128)S(1)}, u32[]{:S(2)}) %copy-start.7) | copy-done | bytes 524312
  21.8 1.1 %slice.28 = f32[1024,128]{1,0:T(8,128)S(1)} slice(f32[1032,128]{1,0:T(8,128)} %collective-permute-done.1), slice={[0:1024], [0:128]} | slice | bytes 1048576 | tf_op jit(solution)/shard_map/slice | solution.py:239
  23.1 1.0 %copy-done.3 = f32[2,8,64,128]{3,2,1,0:T(8,128)S(1)} copy-done((f32[2,8,64,128]{3,2,1,0:T(8,128)S(1)}, f32[2,8,64,128]{3,2,1,0:T(8,128)}, u32[]{:S(2)}) %copy-start.3) | copy-done | bytes 524312
  24.1 1.0 %copy-done.8 = f32[2,8,64,128]{3,2,1,0:T(8,128)S(1)} copy-done((f32[2,8,64,128]{3,2,1,0:T(8,128)S(1)}, f32[2,8,64,128]{3,2,1,0:T(8,128)}, u32[]{:S(2)}) %copy-start.8) | copy-done | bytes 524312
  25.2 2.7 %shard_map.48 = (f32[2,8,64,128]{3,2,1,0:T(8,128)}, f32[2,8,64,128]{3,2,1,0:T(8,128)}) custom-call(s32[1]{0:T(128)} %bitcast.3.refs_0_, bf16[8,3,256,192]{3,2,1,0:T(8,128)(2,1)S(1)} %shard_map.46.refs_0_.refs_1_, f32[2,8,64,128]{3,2,1,0:T(8,128)S(1)} %copy-done.8, f32[2,8,64,128]{3,2,1,0:T(8,128)S(1)} %copy-done.3, f32[2,8,64,128]{3,2,1,0:T(8,128)S(1)} %bitcast.18, ...), custom_call_target="tpu_custom_call" | custom-call | flops 500000000 | bytes 4000000 | tf_op jit(solution)/shard_map/pallas_call | solution.py:198
  27.9 1.3 %collective-permute-start.3 = (f32[2,8,64,128]{3,2,1,0:T(8,128)}, f32[2,8,64,128]{3,2,1,0:T(8,128)}, u32[]{:S(2)}, u32[]{:S(2)}) collective-permute-start(f32[2,8,64,128]{3,2,1,0:T(8,128)} %get-tuple-element.7.refs_3_), channel_id=1, source_target_pairs={{1,0},{3,2},{5,4},{7,6},{9,8},{11,10},{13,12},{15,14},{17,16},{19,... | collective-permute-start | bytes 1572872 | tf_op jit(solution)/shard_map/ppermute | solution.py:211
  29.2 1.3 %collective-permute-start.4 = (f32[2,8,64,128]{3,2,1,0:T(8,128)}, f32[2,8,64,128]{3,2,1,0:T(8,128)}, u32[]{:S(2)}, u32[]{:S(2)}) collective-permute-start(f32[2,8,64,128]{3,2,1,0:T(8,128)} %get-tuple-element.8), channel_id=1, source_target_pairs={{1,2},{3,0},{5,6},{7,4},{9,10},{11,8},{13,14},{15,12},{17,18},{19,... | collective-permute-start | bytes 1572872 | tf_op jit(solution)/shard_map/ppermute | solution.py:211
  30.5 1.3 %collective-permute-start.5 = (f32[2,8,64,128]{3,2,1,0:T(8,128)}, f32[2,8,64,128]{3,2,1,0:T(8,128)}, u32[]{:S(2)}, u32[]{:S(2)}) collective-permute-start(f32[2,8,64,128]{3,2,1,0:T(8,128)} %get-tuple-element.8), channel_id=1, source_target_pairs={{3,4},{5,2},{7,8},{9,6},{11,12},{13,10},{19,20},{21,18},{23,24},{2... | collective-permute-start | bytes 1572872 | tf_op jit(solution)/shard_map/ppermute | solution.py:211
  32.0 13.6 %collective-permute-done.4.refs_4_ = f32[2,8,64,128]{3,2,1,0:T(8,128)} collective-permute-done((f32[2,8,64,128]{3,2,1,0:T(8,128)}, f32[2,8,64,128]{3,2,1,0:T(8,128)}, u32[]{:S(2)}, u32[]{:S(2)}) %collective-permute-start.4) | collective-permute-done | bytes 524320 | tf_op jit(solution)/shard_map/ppermute | solution.py:211
  45.6 1.0 %copy-done.1 = f32[1,2,8,64,128]{4,3,2,1,0:T(8,128)S(1)} copy-done((f32[1,2,8,64,128]{4,3,2,1,0:T(8,128)S(1)}, f32[1,2,8,64,128]{4,3,2,1,0:T(8,128)}, u32[]{:S(2)}) %copy-start.1) | copy-done | bytes 524312
  46.7 1.0 %copy-done.5 = f32[2,8,64,128]{3,2,1,0:T(8,128)S(1)} copy-done((f32[2,8,64,128]{3,2,1,0:T(8,128)S(1)}, f32[2,8,64,128]{3,2,1,0:T(8,128)}, u32[]{:S(2)}) %copy-start.5) | copy-done | bytes 524312
  47.7 2.2 %shard_map.49.refs_2_ = f32[2,8,64,128]{3,2,1,0:T(8,128)S(1)} custom-call(bf16[8,3,256,192]{3,2,1,0:T(8,128)(2,1)S(1)} %shard_map.46.refs_0_.refs_1_, f32[2,8,64,128]{3,2,1,0:T(8,128)S(1)} %bitcast.17, f32[2,8,64,128]{3,2,1,0:T(8,128)S(1)} %copy-done.5, f32[2,8,64,128]{3,2,1,0:T(8,128)} %collective-permute-done.3.refs_3_, ...), custom_call_target="tpu_custom_call" | custom-call | flops 1000000000 | bytes 5000000 | tf_op jit(solution)/shard_map/pallas_call | solution.py:132
  49.9 2.6 %shard_map.50 = f32[2,8,64,128]{3,2,1,0:T(8,128)} custom-call(s32[1]{0:T(128)} %bitcast.refs_0_, bf16[8,3,256,192]{3,2,1,0:T(8,128)(2,1)S(1)} %shard_map.46.refs_0_.refs_1_, f32[2,8,64,128]{3,2,1,0:T(8,128)S(1)} %shard_map.49.refs_2_, f32[2,8,64,128]{3,2,1,0:T(8,128)} %get-tuple-element.7.refs_3_, f32[2,8,64,128]{3,2,1,0:T(8,128)} %collective-permute-done.5.refs_4_), custom_call_target="tpu_custom_call" | custom-call | flops 500000000 | bytes 4000000 | tf_op jit(solution)/shard_map/pallas_call | solution.py:198
  (26 shorter events, 1.5 us)
Async XLA Ops:
  0.0 12.7 %copy-start.9 = (s32[8,9]{1,0:T(8,128)S(1)}, s32[8,9]{1,0:T(8,128)}, u32[]{:S(2)}) copy-start(s32[8,9]{1,0:T(8,128)} %neighbours_ref.1) | copy-start | bytes 868
  2.8 14.7 %collective-permute-start = (f32[2,8,64,128]{3,2,1,0:T(8,128)}, f32[2,8,64,128]{3,2,1,0:T(8,128)}, u32[]{:S(2)}, u32[]{:S(2)}) collective-permute-start(f32[2,8,64,128]{3,2,1,0:T(8,128)} %pad_maximum_fusion.1), channel_id=1, source_target_pairs={{1,3},{3,1},{5,7},{7,5},{9,11},{11,9},{13,15},{15,13},{17,19},{19,... | collective-permute-start | bytes 1572872 | tf_op jit(solution)/shard_map/ppermute | solution.py:211
  6.9 10.6 %copy-start.10 = (f32[2,8,64]{2,1,0:T(8,128)S(1)}, f32[2,8,64]{2,1,0:T(8,128)}, u32[]{:S(2)}) copy-start(f32[2,8,64]{2,1,0:T(8,128)} %param.5) | copy-start | bytes 12292
  6.9 14.1 %collective-permute-start.1 = (f32[1032,128]{1,0:T(8,128)}, f32[1032,128]{1,0:T(8,128)}, u32[]{:S(2)}, u32[]{:S(2)}) collective-permute-start(f32[1032,128]{1,0:T(8,128)} %pad_maximum_fusion), channel_id=1, source_target_pairs={{0,1},{2,3},{4,5},{6,7},{8,9},{10,11},{12,13},{14,15},{16,17},{18,... | collective-permute-start | bytes 1585160 | tf_op jit(solution)/shard_map/ppermute | solution.py:211
  11.2 11.6 %collective-permute-start.2 = (f32[2,8,64,128]{3,2,1,0:T(8,128)}, f32[2,8,64,128]{3,2,1,0:T(8,128)}, u32[]{:S(2)}, u32[]{:S(2)}) collective-permute-start(f32[2,8,64,128]{3,2,1,0:T(8,128)} %pad_maximum_fusion.1), channel_id=1, source_target_pairs={{3,5},{5,3},{7,9},{9,7},{11,13},{13,11},{19,21},{21,19},{23,25},{2... | collective-permute-start | bytes 1572872 | tf_op jit(solution)/shard_map/ppermute | solution.py:211
  12.7 1.7 %copy-start.6 = (f32[8,2,64,576]{3,2,1,0:T(8,128)S(1)}, f32[8,2,64,576]{3,2,1,0:T(8,128)}, u32[]{:S(2)}) copy-start(f32[8,2,64,576]{3,2,1,0:T(8,128)} %block_ref.1) | copy-start | bytes 7077892
  14.4 3.4 %copy-start = (f32[1,2,8,64,128]{4,3,2,1,0:T(8,128)S(1)}, f32[1,2,8,64,128]{4,3,2,1,0:T(8,128)}, u32[]{:S(2)}) copy-start(f32[1,2,8,64,128]{4,3,2,1,0:T(8,128)} %param.4) | copy-start | bytes 1572868
  17.7 2.5 %copy-start.4 = (f32[2,8,64,128]{3,2,1,0:T(8,128)}, f32[2,8,64,128]{3,2,1,0:T(8,128)S(1)}, u32[]{:S(2)}) copy-start(f32[2,8,64,128]{3,2,1,0:T(8,128)S(1)} %broadcast_in_dim.39.refs_2_) | copy-start | bytes 1572868
  17.8 2.4 %copy-start.2 = (f32[2,8,64,128]{3,2,1,0:T(8,128)}, f32[2,8,64,128]{3,2,1,0:T(8,128)S(1)}, u32[]{:S(2)}) copy-start(f32[2,8,64,128]{3,2,1,0:T(8,128)S(1)} %broadcast_in_dim.42.refs_3_) | copy-start | bytes 1572868
  20.2 0.8 %copy-start.7 = (f32[2,8,64,128]{3,2,1,0:T(8,128)}, f32[2,8,64,128]{3,2,1,0:T(8,128)S(1)}, u32[]{:S(2)}) copy-start(f32[2,8,64,128]{3,2,1,0:T(8,128)S(1)} %shard_map.47.refs_2_) | copy-start | bytes 1572868
  23.1 1.0 %copy-start.3 = (f32[2,8,64,128]{3,2,1,0:T(8,128)S(1)}, f32[2,8,64,128]{3,2,1,0:T(8,128)}, u32[]{:S(2)}) copy-start(f32[2,8,64,128]{3,2,1,0:T(8,128)} %copy-done.2) | copy-start | bytes 1572868
  24.1 1.0 %copy-start.8 = (f32[2,8,64,128]{3,2,1,0:T(8,128)S(1)}, f32[2,8,64,128]{3,2,1,0:T(8,128)}, u32[]{:S(2)}) copy-start(f32[2,8,64,128]{3,2,1,0:T(8,128)} %copy-done.7) | copy-start | bytes 1572868
  27.9 4.1 %collective-permute-start.3 = (f32[2,8,64,128]{3,2,1,0:T(8,128)}, f32[2,8,64,128]{3,2,1,0:T(8,128)}, u32[]{:S(2)}, u32[]{:S(2)}) collective-permute-start(f32[2,8,64,128]{3,2,1,0:T(8,128)} %get-tuple-element.7.refs_3_), channel_id=1, source_target_pairs={{1,0},{3,2},{5,4},{7,6},{9,8},{11,10},{13,12},{15,14},{17,16},{19,... | collective-permute-start | bytes 1572872 | tf_op jit(solution)/shard_map/ppermute | solution.py:211
  29.2 16.4 %collective-permute-start.4 = (f32[2,8,64,128]{3,2,1,0:T(8,128)}, f32[2,8,64,128]{3,2,1,0:T(8,128)}, u32[]{:S(2)}, u32[]{:S(2)}) collective-permute-start(f32[2,8,64,128]{3,2,1,0:T(8,128)} %get-tuple-element.8), channel_id=1, source_target_pairs={{1,2},{3,0},{5,6},{7,4},{9,10},{11,8},{13,14},{15,12},{17,18},{19,... | collective-permute-start | bytes 1572872 | tf_op jit(solution)/shard_map/ppermute | solution.py:211
  30.5 19.4 %collective-permute-start.5 = (f32[2,8,64,128]{3,2,1,0:T(8,128)}, f32[2,8,64,128]{3,2,1,0:T(8,128)}, u32[]{:S(2)}, u32[]{:S(2)}) collective-permute-start(f32[2,8,64,128]{3,2,1,0:T(8,128)} %get-tuple-element.8), channel_id=1, source_target_pairs={{3,4},{5,2},{7,8},{9,6},{11,12},{13,10},{19,20},{21,18},{23,24},{2... | collective-permute-start | bytes 1572872 | tf_op jit(solution)/shard_map/ppermute | solution.py:211
  45.6 1.0 %copy-start.1 = (f32[1,2,8,64,128]{4,3,2,1,0:T(8,128)S(1)}, f32[1,2,8,64,128]{4,3,2,1,0:T(8,128)}, u32[]{:S(2)}) copy-start(f32[1,2,8,64,128]{4,3,2,1,0:T(8,128)} %param.4) | copy-start | bytes 1572868
  46.7 1.0 %copy-start.5 = (f32[2,8,64,128]{3,2,1,0:T(8,128)S(1)}, f32[2,8,64,128]{3,2,1,0:T(8,128)}, u32[]{:S(2)}) copy-start(f32[2,8,64,128]{3,2,1,0:T(8,128)} %copy-done.4) | copy-start | bytes 1572868

commit v2 on v0

v2 whole, which is shorter than its diff:
```python
import functools

import jax
import jax.numpy as jnp
from jax import lax
from jax.experimental import pallas as pl
from jax.experimental.pallas import tpu as pltpu
from jax.sharding import PartitionSpec as P

N_LAT = 8
DIRECT = 8
EXTRA = 8
VMEM = pl.BlockSpec(memory_space=pltpu.VMEM)
SMEM = pl.BlockSpec(memory_space=pltpu.SMEM)
HBM = pl.BlockSpec(memory_space=pltpu.HBM)
LIMIT = 24 * 1024 * 1024


def split(value):
    high = value.astype(jnp.bfloat16)
    low = (value - high.astype(jnp.float32)).astype(jnp.bfloat16)
    return high, low


def arrange_kernel(strip_ref, neighbours_ref, block_ref, out_ref, neighbours, held, tail, slot_of, index_load, loads):
    tiles, _, points, inputs = block_ref.shape
    width = 2 * points
    copies = [pltpu.make_async_copy(block_ref.at[t], held.at[t], loads.at[t]) for t in range(tiles)]
    copy_index = pltpu.make_async_copy(neighbours_ref, neighbours, index_load.at[0])
    copy_index.start()
    for copy in copies:
        copy.start()
    copy_index.wait()
    strip = strip_ref[0]
    near = 1 - 2 * lax.rem(strip, 2)
    for t in range(tiles):
        for k in range(9):
            slot_of[t * 10 + k] = -1
        for s in range(9):
            index = neighbours[t, s]
            safe = jnp.maximum(index, 0)
            offset = lax.div(safe, tiles) - strip
            column = lax.rem(safe, tiles) - t + 1
            group = jnp.where(offset == 0, 0, jnp.where(offset == near, 1, 2))
            slot_of[t * 10 + jnp.where(index >= 0, group * 3 + column, 9)] = s
    lane = lax.broadcasted_iota(jnp.int32, (points, width), 1)

    def one_tile(t, carry):
        pltpu.make_async_copy(block_ref.at[t], held.at[t], loads.at[t]).wait()
        tail[:, :, :points] = held[t, :, :, 8 * points :]
        for group in range(3):
            found = [slot_of[t * 10 + group * 3 + j] for j in range(3)]
            safe = [jnp.maximum(s, 0) for s in found]
            for part in range(2):
                loaded = []
                for j in range(3):
                    start = pl.multiple_of(jnp.minimum(lax.div(safe[j], 2), 3) * width, width)
                    value = jnp.where(safe[j] == 8, tail[part], held[t, part, :, pl.ds(start, width)])
                    value = jnp.where(lax.rem(safe[j] + j, 2) == 0, value, pltpu.roll(value, points, 1))
                    loaded.append(jnp.where(found[j] >= 0, value, 0.0))
                first = jnp.where(lane < points, loaded[0], loaded[1])
                for at, value in ((0, first), (width, loaded[2][:, :points])):
                    high, low = split(value)
                    columns = slice(at, at + value.shape[1])
                    out_ref[t, group, part * points : (part + 1) * points, columns] = high
                    out_ref[t, group, (2 + part) * points : (3 + part) * points, columns] = low
        return carry

    lax.fori_loop(0, tiles, one_tile, 0)


def arrange(strip, neighbours, extrapolator):
    tiles, _, points, inputs = extrapolator.shape
    return pl.pallas_call(
        arrange_kernel,
        in_specs=[SMEM, HBM, HBM],
        out_specs=VMEM,
        out_shape=jax.ShapeDtypeStruct((tiles, 3, 4 * points, 3 * points), jnp.bfloat16),
        scratch_shapes=[
            pltpu.SMEM(neighbours.shape, jnp.int32),
            pltpu.VMEM(extrapolator.shape, jnp.float32),
            pltpu.VMEM((2, points, 2 * points), jnp.float32),
            pltpu.SMEM((10 * tiles,), jnp.int32),
            pltpu.SemaphoreType.DMA((1,)),
            pltpu.SemaphoreType.DMA((tiles,)),
        ],
        **params(4_000_000, 6_000_000),
    )(strip, in_hbm(neighbours), in_hbm(extrapolator))


def transmitted(source, transmit, incoming):
    factor = 1.0 + transmit[0]
    return (
        factor * incoming[0] - transmit[1] * incoming[1] + source[0],
        factor * incoming[1] + transmit[1] * incoming[0] + source[1],
    )


def columns_of(transmit, square):
    parts, tiles, points = transmit.shape
    square[...] = jnp.zeros_like(square)
    square[: parts * tiles, :points] = transmit.reshape(parts * tiles, points)
    square[...] = square[...].T


def wide(square, tile, tiles, points, shots):
    return [
        jnp.broadcast_to(square[:points, p * tiles + tile : p * tiles + tile + 1], (points, shots)) for p in range(2)
    ]


def product(blocks, high_ref, low_ref, tile, points):
    rows = slice(tile * points, (tile + 3) * points)
    first = jnp.dot(blocks, high_ref[rows], preferred_element_type=jnp.float32)
    second = jnp.dot(blocks[: 2 * points], low_ref[rows], preferred_element_type=jnp.float32)
    return first[: 2 * points] + (first[2 * points :] + second)


def complex_parts(four, points, shots):
    real = four[:points, :shots] - four[points:, shots:]
    imaginary = four[:points, shots:] + four[points:, :shots]
    return real, imaginary


def copies_in(refs, held, semaphores):
    copies, at = [], 0
    for k, ref in enumerate(refs):
        rows = ref.shape[1] - EXTRA
        copies.append(pltpu.make_async_copy(ref.at[:, :rows], held.at[:, at : at + rows], semaphores.at[k]))
        at += rows
    return copies


def copies_out(refs, held, semaphores):
    copies, at = [], 0
    for k, ref in enumerate(refs):
        rows = ref.shape[1] - EXTRA
        copy = pltpu.make_async_copy(held.at[:, at : at + rows], ref.at[:, :rows], semaphores.at[k])
        at += rows
        copies.append((at, copy))
    return copies


def in_hbm(value):
    return pltpu.with_memory_space_constraint(value, pltpu.HBM)


def params(flops, copied):
    return dict(
        compiler_params=pltpu.CompilerParams(vmem_limit_bytes=LIMIT),
        cost_estimate=pl.CostEstimate(flops=flops, bytes_accessed=copied, transcendentals=0),
    )


def pieces_like(field, counts):
    _, _, points, shots = field.shape
    return [jax.ShapeDtypeStruct((2, count * points + EXTRA, shots), jnp.float32) for count in counts]


def field_scratch(field):
    return pltpu.VMEM(field.shape, jnp.float32)


def flat_scratch(field):
    _, tiles, points, shots = field.shape
    return pltpu.VMEM((2, tiles * points, shots), jnp.float32)


def split_scratch(field):
    _, tiles, points, shots = field.shape
    return [pltpu.VMEM(((tiles + 2) * points, 2 * shots), jnp.bfloat16)] * 2


def transmit_scratch(field):
    return [pltpu.VMEM((2, *field.shape[1:3]), jnp.float32), pltpu.VMEM((128, 128), jnp.float32)]


def first_kernel(counts, packs, source_ref, transmit_ref, *refs):
    sent_refs, refs = refs[: len(counts)], refs[len(counts) :]
    if packs:
        packed_ref, refs = refs[0], refs[1:]
    held, made, transmit, square, loads, stores = refs[:6]
    _, tiles, points, shots = held.shape
    copy_transmit = pltpu.make_async_copy(transmit_ref, transmit, loads.at[1])
    copy_source = pltpu.make_async_copy(source_ref, held, loads.at[0])
    copy_transmit.start()
    copy_source.start()
    outgoing = copies_out(sent_refs, made, stores)
    copy_transmit.wait()
    columns_of(transmit[...], square)
    if packs:
        beside, pack_stores = refs[6:]
        beside[...] = jnp.zeros_like(beside)
        for part in range(2):
            beside[part, :, :tiles] = square[:points, part * tiles : (part + 1) * tiles]
        pack = pltpu.make_async_copy(beside, packed_ref, pack_stores.at[0])
        pack.start()
    copy_source.wait()
    start_field = jnp.zeros((points, shots), jnp.float32)
    for t in range(tiles):
        rows = slice(t * points, (t + 1) * points)
        made[0, rows], made[1, rows] = transmitted(
            (held[0, t], held[1, t]), wide(square, t, tiles, points, shots), (start_field, start_field)
        )
        for ready, copy in outgoing:
            if ready == rows.stop:
                copy.start()
    if packs:
        pack.wait()
    for _, copy in outgoing:
        copy.wait()


def first_field(source, transmit, counts, packs):
    _, _, points, shots = source.shape
    shapes = pieces_like(source, counts)
    scratch = [
        field_scratch(source),
        flat_scratch(source),
        *transmit_scratch(source),
        pltpu.SemaphoreType.DMA((2,)),
        pltpu.SemaphoreType.DMA((len(counts),)),
    ]
    if packs:
        shapes.append(jax.ShapeDtypeStruct((2, points, shots), jnp.float32))
        scratch += [pltpu.VMEM((2, points, shots), jnp.float32), pltpu.SemaphoreType.DMA((1,))]
    return pl.pallas_call(
        functools.partial(first_kernel, counts, packs),
        in_specs=[HBM, HBM],
        out_specs=[HBM] * len(shapes),
        out_shape=shapes,
        scratch_shapes=scratch,
        **params(500_000_000, 4_000_000),
    )(in_hbm(source), in_hbm(transmit))


def convert(value, high_ref, low_ref, t):
    points, shots = value[0].shape
    for part in range(2):
        high, low = split(value[part])
        rows = slice((1 + t) * points, (2 + t) * points)
        high_ref[rows, part * shots : (part + 1) * shots] = high
        low_ref[rows, part * shots : (part + 1) * shots] = low


def clear_ends(high_ref, low_ref, points):
    for ref in (high_ref, low_ref):
        rows = ref.shape[0]
        zero = jnp.zeros((points, ref.shape[1]), ref.dtype)
        ref[0:points] = zero
        ref[rows - points : rows] = zero


def own_kernel(first, active_ref, blocks_ref, transmit_ref, source_ref, *refs):
    if not first:
        came_ref, refs = refs[0], refs[1:]
    out_ref, source, came, high_ref, low_ref, transmit, square, loads = refs
    _, tiles, points, shots = out_ref.shape

    @pl.when(active_ref[0] > 0)
    def _():
        copies = [
            pltpu.make_async_copy(transmit_ref, transmit, loads.at[0]),
            pltpu.make_async_copy(source_ref, source, loads.at[1]),
        ]
        if not first:
            copies.append(pltpu.make_async_copy(came_ref, came, loads.at[2]))
        for copy in copies:
            copy.start()
        clear_ends(high_ref, low_ref, points)
        for copy in copies:
            copy.wait()
        columns_of(transmit[...], square)
        zero = jnp.zeros((points, shots), jnp.float32)
        for t in range(tiles):
            field = (zero, zero) if first else (came[0, t], came[1, t])
            value = transmitted((source[0, t], source[1, t]), wide(square, t, tiles, points, shots), field)
            convert(value, high_ref, low_ref, t)
        for t in range(tiles):
            four = product(blocks_ref[t, 0], high_ref, low_ref, t, points)
            out_ref[0, t], out_ref[1, t] = complex_parts(four, points, shots)


def own_sum(active, blocks, transmit, source, came):
    values = [transmit, source] if came is None else [transmit, source, came]
    return pl.pallas_call(
        functools.partial(own_kernel, came is None),
        in_specs=[SMEM, VMEM] + [HBM] * len(values),
        out_specs=VMEM,
        out_shape=jax.ShapeDtypeStruct(source.shape, jnp.float32),
        scratch_shapes=[
            field_scratch(source),
            field_scratch(source),
            *split_scratch(source),
            *transmit_scratch(source),
            pltpu.SemaphoreType.DMA((3,)),
        ],
        **params(*((500_000_000, 2_000_000) if came is None else (1_000, 1_000))),
    )(active, blocks, *map(in_hbm, values))


def rest_kernel(first, near_pieces, far_pieces, counts, active_ref, blocks_ref, partial_ref, *refs):
    if not first:
        refs = refs[1:]
    if counts:
        factor_ref, source_ref, refs = refs[0], refs[1], refs[2:]
    near_refs, refs = refs[:near_pieces], refs[near_pieces:]
    far_refs, refs = refs[:far_pieces], refs[far_pieces:]
    out_ref, sent_refs, refs = refs[0], refs[1 : 1 + len(counts)], refs[1 + len(counts) :]
    near, far, made, near_high, near_low, far_high, far_low, near_loads, far_loads, stores = refs[:10]
    if counts:
        factor, source, sent, more_loads, more_stores = refs[10:]
    _, tiles, points, shots = out_ref.shape

    @pl.when(active_ref[0] > 0)
    def _():
        copies = copies_in(near_refs, near, near_loads) + copies_in(far_refs, far, far_loads)
        if counts:
            copies.append(pltpu.make_async_copy(factor_ref, factor, more_loads.at[0]))
            copies.append(pltpu.make_async_copy(source_ref, source, more_loads.at[1]))
            outgoing = copies_out(sent_refs, sent, more_stores)
        for copy in copies:
            copy.start()
        clear_ends(near_high, near_low, points)
        clear_ends(far_high, far_low, points)
        for copy in copies:
            copy.wait()
        half = tiles // 2
        results = [
            (half, pltpu.make_async_copy(made.at[:, :half], out_ref.at[:, :half], stores.at[0])),
            (tiles, pltpu.make_async_copy(made.at[:, half:], out_ref.at[:, half:], stores.at[1])),
        ]
        for t in range(tiles):
            rows = slice(t * points, (t + 1) * points)
            convert((near[0, rows], near[1, rows]), near_high, near_low, t)
            convert((far[0, rows], far[1, rows]), far_high, far_low, t)
        for t in range(tiles):
            four = product(blocks_ref[t, 1], near_high, near_low, t, points)
            four += product(blocks_ref[t, 2], far_high, far_low, t, points)
            real, imaginary = complex_parts(four, points, shots)
            real += partial_ref[0, t]
            imaginary += partial_ref[1, t]
            made[0, t] = real
            made[1, t] = imaginary
            if counts:
                rows = slice(t * points, (t + 1) * points)
                factors = [jnp.broadcast_to(factor[p, :, t : t + 1], (points, shots)) for p in range(2)]
                sent[0, rows], sent[1, rows] = transmitted((source[0, t], source[1, t]), factors, (real, imaginary))
                for ready, copy in outgoing:
                    if ready == rows.stop:
                        copy.start()
            for ready, copy in results:
                if ready == t + 1:
                    copy.start()
        for _, copy in results + (outgoing if counts else []):
            copy.wait()


def rest_sum(active, blocks, partial, before, below, near, far, counts):
    shapes = [jax.ShapeDtypeStruct(partial.shape, jnp.float32)] + pieces_like(partial, counts)
    scratch = [flat_scratch(partial)] * 2 + [field_scratch(partial)] + split_scratch(partial) * 2
    scratch += [pltpu.SemaphoreType.DMA((count,)) for count in (len(near), len(far), 2)]
    specs, values, aliases = [SMEM, VMEM, VMEM], [active, blocks, partial], {}
    if before is not None:
        specs += [HBM]
        values += [in_hbm(before)]
        aliases = {3: 0}
    if counts:
        specs += [pl.BlockSpec(memory_space=pl.ANY), HBM]
        values += [below[0], in_hbm(below[1])]
        scratch += [
            field_scratch(below[0]),
            field_scratch(partial),
            flat_scratch(partial),
            pltpu.SemaphoreType.DMA((2,)),
            pltpu.SemaphoreType.DMA((len(counts),)),
        ]
    return pl.pallas_call(
        functools.partial(rest_kernel, before is None, len(near), len(far), counts),
        in_specs=specs + [HBM] * (len(near) + len(far)),
        out_specs=[HBM] * len(shapes),
        out_shape=shapes,
        scratch_shapes=scratch,
        input_output_aliases=aliases,
        **params(1_000_000_000, 4_000_000),
    )(*values, *map(in_hbm, near + far))


def send(value, route):
    return lax.ppermute(value, "depth", route)


def body(source, transmit, neighbours, extrapolator):
    field = source[0]
    tiles = field.shape[1]
    levels = lax.axis_size("depth") // N_LAT
    place = lax.axis_index("depth")
    strip = place // levels
    level = levels - 1 - place % levels
    strips = range(N_LAT)
    pieces = (DIRECT, tiles - DIRECT) if DIRECT < tiles else (tiles,)
    more = levels > 1

    def at(s, n):
        return s * levels + levels - 1 - n

    def far_of(s):
        return s + 1 if s % 2 else s - 1

    sent = first_field(field, transmit, pieces, more)
    (*sent,), extrapolator = lax.optimization_barrier((sent, extrapolator))
    blocks = arrange(strip[None], neighbours, extrapolator)
    below = None
    if more:
        *below, _ = lax.optimization_barrier((sent.pop(), field, blocks))
        below = [send(b, [(p, p + 1) for p in range(N_LAT * levels) if (p + 1) % levels]) for b in below]
    output = None
    for n in range(levels):
        m = max(n - 1, 0)
        active = (level == n).astype(jnp.int32)[None]
        with_far = [s for s in strips if far_of(s) in strips]
        near = [send(piece, [(at(s, m), at(s ^ 1, n)) for s in strips]) for piece in sent[::-1]][::-1]
        far = [send(sent[0], [(at(s, m), at(far_of(s), n)) for s in with_far])]
        if len(sent) > 1:
            far.append(send(near[1], [(at(s ^ 1, n), at(far_of(s), n)) for s in with_far]))
        came = send(output, [(at(s, m), at(s, n)) for s in strips]) if n else None
        partial = own_sum(active, blocks, transmit, field, came)
        counts = () if n == levels - 1 else (tiles,)
        output, *sent = rest_sum(active, blocks, partial, output, below, near, far, counts)
    return output[None]


def solution(mesh):
    in_specs = (
        P("groups", None, "depth", None, None),
        P(None, "depth", None),
        P("depth", None),
        P("depth", None, None, None),
    )
    out_specs = P("groups", None, "depth", None, None)
    return jax.shard_map(body, mesh=mesh, in_specs=in_specs, out_specs=out_specs, check_vma=False)
```

time: 112 us -> 40.9 us (0.37)
  the two profiles are of different devices: /device:TPU:19 before, /device:TPU:24 now
where the time goes in v2:
time: 40.9 us; the launch traced here: 40.4 us
  waiting for transfers between devices  17.1 us (42%)
  starting transfers between devices  12.7 us (31%)
  Pallas kernels  10.5 us (26%)
    ppermute x7, waiting for transfers between devices, send(): return lax.ppermute(value, 'depth', route)  17.1 us
    ppermute x7, starting transfers between devices, send(): return lax.ppermute(value, 'depth', route)  12.7 us
    pallas_call x1, Pallas kernels, arrange(): pl.pallas_call(arrange_kernel, in_specs=[SMEM, HBM, HBM], out_specs=VMEM,...  3.28 us
    pallas_call x2, Pallas kernels, rest_sum(): pl.pallas_call(functools.partial(rest_kernel, before is None, len(near),...  3 us
    pallas_call x1, Pallas kernels, first_field(): pl.pallas_call(functools.partial(first_kernel, counts, packs), in_specs=[...  2.12 us
    pallas_call x2, Pallas kernels, own_sum(): pl.pallas_call(functools.partial(own_kernel, came is None), in_specs=[SME...  2.07 us
  transfers between devices with their start and end apart: 7, of which 4 were waited for; matrix products, arithmetic and copies ran while one was open for 0% of the time, Pallas kernels for 13%

profile of v2, /device:TPU:24, one launch (start us, length us, event | category | flops | bytes accessed | tf_op | source)
XLA Modules:
  0.0 40.4 jit_solution(8302099013636058340)
XLA Ops:
  0.0 2.1 %shard_map.46 = (f32[2,520,128]{2,1,0:T(8,128)}, f32[2,64,128]{2,1,0:T(8,128)S(1)}) custom-call(f32[2,8,64,128]{3,2,1,0:T(8,128)} %bitcast.5, f32[2,8,64]{2,1,0:T(8,128)} %transmit_ref.5), custom_call_target="tpu_custom_call" | custom-call | flops 500000000 | bytes 4000000 | tf_op jit(solution)/shard_map/pallas_call | solution.py:227
  2.1 1.5 %collective-permute-start.3 = (f32[2,520,128]{2,1,0:T(8,128)}, f32[2,520,128]{2,1,0:T(8,128)}, u32[]{:S(2)}, u32[]{:S(2)}) collective-permute-start(f32[2,520,128]{2,1,0:T(8,128)} %get-tuple-element.20), channel_id=1, source_target_pairs={{3,5},{5,3},{7,9},{9,7},{11,13},{13,11},{19,21},{21,19},{23,25},{2... | collective-permute-start | bytes 1597448 | tf_op jit(solution)/shard_map/ppermute | solution.py:390
  3.6 1.4 %collective-permute-start.2 = (f32[2,520,128]{2,1,0:T(8,128)}, f32[2,520,128]{2,1,0:T(8,128)}, u32[]{:S(2)}, u32[]{:S(2)}) collective-permute-start(f32[2,520,128]{2,1,0:T(8,128)} %get-tuple-element.20), channel_id=1, source_target_pairs={{1,3},{3,1},{5,7},{7,5},{9,11},{11,9},{13,15},{15,13},{17,19},{19,... | collective-permute-start | bytes 1597448 | tf_op jit(solution)/shard_map/ppermute | solution.py:390
  5.1 3.3 %shard_map.47.blocks_ref = bf16[8,3,256,192]{3,2,1,0:T(8,128)(2,1)S(1)} custom-call(s32[1]{0:T(128)} %bitcast.1.strip_ref, s32[8,9]{1,0:T(8,128)} %neighbours_ref.1, f32[8,2,64,576]{3,2,1,0:T(8,128)} %block_ref), custom_call_target="tpu_custom_call" | custom-call | flops 4000000 | bytes 6000000 | tf_op jit(solution)/shard_map/pallas_call | solution.py:74
  8.4 4.6 %collective-permute-start.1 = (f32[2,8,64,128]{3,2,1,0:T(8,128)}, f32[2,8,64,128]{3,2,1,0:T(8,128)}, u32[]{:S(2)}, u32[]{:S(2)}) collective-permute-start(f32[2,8,64,128]{3,2,1,0:T(8,128)} %bitcast.6), channel_id=1, source_target_pairs={{0,1},{2,3},{4,5},{6,7},{8,9},{10,11},{12,13},{14,15},{16,17},{18,... | collective-permute-start | bytes 1572872 | tf_op jit(solution)/shard_map/ppermute | solution.py:390
  12.9 1.3 %collective-permute-start = (f32[2,64,128]{2,1,0:T(8,128)S(1)}, f32[2,64,128]{2,1,0:T(8,128)S(1)}, u32[]{:S(2)}, u32[]{:S(2)}) collective-permute-start(f32[2,64,128]{2,1,0:T(8,128)S(1)} %get-tuple-element.18), channel_id=1, source_target_pairs={{0,1},{2,3},{4,5},{6,7},{8,9},{10,11},{12,13},{14,15},{16,17},{18,... | collective-permute-start | bytes 196616 | tf_op jit(solution)/shard_map/ppermute | solution.py:390
  14.3 0.8 %collective-permute-done.refs_0_ = f32[2,64,128]{2,1,0:T(8,128)S(1)} collective-permute-done((f32[2,64,128]{2,1,0:T(8,128)S(1)}, f32[2,64,128]{2,1,0:T(8,128)S(1)}, u32[]{:S(2)}, u32[]{:S(2)}) %collective-permute-start) | collective-permute-done | bytes 65568 | tf_op jit(solution)/shard_map/ppermute | solution.py:390
  15.1 0.0 collective-permute-done.1.refs_1_
  15.1 0.0 collective-permute-done.3.refs_3_
  15.1 0.0 collective-permute-done.2.refs_2_
  15.1 0.1 shard_map.49
  15.2 1.3 %collective-permute-start.6 = (f32[2,520,128]{2,1,0:T(8,128)}, f32[2,520,128]{2,1,0:T(8,128)}, u32[]{:S(2)}, u32[]{:S(2)}) collective-permute-start(f32[2,520,128]{2,1,0:T(8,128)} %get-tuple-element.22), channel_id=1, source_target_pairs={{3,4},{5,2},{7,8},{9,6},{11,12},{13,10},{19,20},{21,18},{23,24},{2... | collective-permute-start | bytes 1597448 | tf_op jit(solution)/shard_map/ppermute | solution.py:390
  16.5 1.3 %collective-permute-start.5 = (f32[2,520,128]{2,1,0:T(8,128)}, f32[2,520,128]{2,1,0:T(8,128)}, u32[]{:S(2)}, u32[]{:S(2)}) collective-permute-start(f32[2,520,128]{2,1,0:T(8,128)} %get-tuple-element.22), channel_id=1, source_target_pairs={{1,2},{3,0},{5,6},{7,4},{9,10},{11,8},{13,14},{15,12},{17,18},{19,... | collective-permute-start | bytes 1597448 | tf_op jit(solution)/shard_map/ppermute | solution.py:390
  17.8 1.3 %collective-permute-start.4 = (f32[2,8,64,128]{3,2,1,0:T(8,128)}, f32[2,8,64,128]{3,2,1,0:T(8,128)}, u32[]{:S(2)}, u32[]{:S(2)}) collective-permute-start(f32[2,8,64,128]{3,2,1,0:T(8,128)} %get-tuple-element.21.refs_0_), channel_id=1, source_target_pairs={{1,0},{3,2},{5,4},{7,6},{9,8},{11,10},{13,12},{15,14},{17,16},{19,... | collective-permute-start | bytes 1572872 | tf_op jit(solution)/shard_map/ppermute | solution.py:390
  19.1 10.4 %collective-permute-done.4.refs_0_ = f32[2,8,64,128]{3,2,1,0:T(8,128)} collective-permute-done((f32[2,8,64,128]{3,2,1,0:T(8,128)}, f32[2,8,64,128]{3,2,1,0:T(8,128)}, u32[]{:S(2)}, u32[]{:S(2)}) %collective-permute-start.4) | collective-permute-done | bytes 524320 | tf_op jit(solution)/shard_map/ppermute | solution.py:390
  29.5 2.0 %shard_map.50.partial_ref = f32[2,8,64,128]{3,2,1,0:T(8,128)S(1)} custom-call(s32[1]{0:T(128)} %bitcast.active_ref, bf16[8,3,256,192]{3,2,1,0:T(8,128)(2,1)S(1)} %shard_map.47.blocks_ref, f32[2,8,64]{2,1,0:T(8,128)} %transmit_ref.5, f32[2,8,64,128]{3,2,1,0:T(8,128)} %bitcast.8, f32[2,8,64,128]{3,2,1,0:T(8,128)} %collective-permute-done.4.refs_0_), custom_call_target="tpu_custom_call" | custom-call | flops 1000 | bytes 1000 | tf_op jit(solution)/shard_map/pallas_call | solution.py:286
  31.5 0.4 collective-permute-done.6.refs_2_
  31.9 5.6 %collective-permute-done.5.refs_1_ = f32[2,520,128]{2,1,0:T(8,128)} collective-permute-done((f32[2,520,128]{2,1,0:T(8,128)}, f32[2,520,128]{2,1,0:T(8,128)}, u32[]{:S(2)}, u32[]{:S(2)}) %collective-permute-start.5) | collective-permute-done | bytes 532512 | tf_op jit(solution)/shard_map/ppermute | solution.py:390
  37.4 2.9 %shard_map.51 = f32[2,8,64,128]{3,2,1,0:T(8,128)} custom-call(s32[1]{0:T(128)} %bitcast.active_ref, bf16[8,3,256,192]{3,2,1,0:T(8,128)(2,1)S(1)} %shard_map.47.blocks_ref, f32[2,8,64,128]{3,2,1,0:T(8,128)S(1)} %shard_map.50.partial_ref, f32[2,8,64,128]{3,2,1,0:T(8,128)} %get-tuple-element.21.refs_0_, ...), custom_call_target="tpu_custom_call", output_to_operand_aliasing={{}: (3, {})} | custom-call | flops 1000000000 | bytes 4000000 | tf_op jit(solution)/shard_map/pallas_call | solution.py:378
  (1 shorter events, 0.0 us)
Async XLA Ops:
  2.1 13.0 %collective-permute-start.3 = (f32[2,520,128]{2,1,0:T(8,128)}, f32[2,520,128]{2,1,0:T(8,128)}, u32[]{:S(2)}, u32[]{:S(2)}) collective-permute-start(f32[2,520,128]{2,1,0:T(8,128)} %get-tuple-element.20), channel_id=1, source_target_pairs={{3,5},{5,3},{7,9},{9,7},{11,13},{13,11},{19,21},{21,19},{23,25},{2... | collective-permute-start | bytes 1597448 | tf_op jit(solution)/shard_map/ppermute | solution.py:390
  3.6 11.5 %collective-permute-start.2 = (f32[2,520,128]{2,1,0:T(8,128)}, f32[2,520,128]{2,1,0:T(8,128)}, u32[]{:S(2)}, u32[]{:S(2)}) collective-permute-start(f32[2,520,128]{2,1,0:T(8,128)} %get-tuple-element.20), channel_id=1, source_target_pairs={{1,3},{3,1},{5,7},{7,5},{9,11},{11,9},{13,15},{15,13},{17,19},{19,... | collective-permute-start | bytes 1597448 | tf_op jit(solution)/shard_map/ppermute | solution.py:390
  8.4 6.7 %collective-permute-start.1 = (f32[2,8,64,128]{3,2,1,0:T(8,128)}, f32[2,8,64,128]{3,2,1,0:T(8,128)}, u32[]{:S(2)}, u32[]{:S(2)}) collective-permute-start(f32[2,8,64,128]{3,2,1,0:T(8,128)} %bitcast.6), channel_id=1, source_target_pairs={{0,1},{2,3},{4,5},{6,7},{8,9},{10,11},{12,13},{14,15},{16,17},{18,... | collective-permute-start | bytes 1572872 | tf_op jit(solution)/shard_map/ppermute | solution.py:390
  12.9 2.2 %collective-permute-start = (f32[2,64,128]{2,1,0:T(8,128)S(1)}, f32[2,64,128]{2,1,0:T(8,128)S(1)}, u32[]{:S(2)}, u32[]{:S(2)}) collective-permute-start(f32[2,64,128]{2,1,0:T(8,128)S(1)} %get-tuple-element.18), channel_id=1, source_target_pairs={{0,1},{2,3},{4,5},{6,7},{8,9},{10,11},{12,13},{14,15},{16,17},{18,... | collective-permute-start | bytes 196616 | tf_op jit(solution)/shard_map/ppermute | solution.py:390
  15.2 16.7 %collective-permute-start.6 = (f32[2,520,128]{2,1,0:T(8,128)}, f32[2,520,128]{2,1,0:T(8,128)}, u32[]{:S(2)}, u32[]{:S(2)}) collective-permute-start(f32[2,520,128]{2,1,0:T(8,128)} %get-tuple-element.22), channel_id=1, source_target_pairs={{3,4},{5,2},{7,8},{9,6},{11,12},{13,10},{19,20},{21,18},{23,24},{2... | collective-permute-start | bytes 1597448 | tf_op jit(solution)/shard_map/ppermute | solution.py:390
  16.5 21.0 %collective-permute-start.5 = (f32[2,520,128]{2,1,0:T(8,128)}, f32[2,520,128]{2,1,0:T(8,128)}, u32[]{:S(2)}, u32[]{:S(2)}) collective-permute-start(f32[2,520,128]{2,1,0:T(8,128)} %get-tuple-element.22), channel_id=1, source_target_pairs={{1,2},{3,0},{5,6},{7,4},{9,10},{11,8},{13,14},{15,12},{17,18},{19,... | collective-permute-start | bytes 1597448 | tf_op jit(solution)/shard_map/ppermute | solution.py:390
  17.8 11.7 %collective-permute-start.4 = (f32[2,8,64,128]{3,2,1,0:T(8,128)}, f32[2,8,64,128]{3,2,1,0:T(8,128)}, u32[]{:S(2)}, u32[]{:S(2)}) collective-permute-start(f32[2,8,64,128]{3,2,1,0:T(8,128)} %get-tuple-element.21.refs_0_), channel_id=1, source_target_pairs={{1,0},{3,2},{5,4},{7,6},{9,8},{11,10},{13,12},{15,14},{17,16},{19,... | collective-permute-start | bytes 1572872 | tf_op jit(solution)/shard_map/ppermute | solution.py:390

commit v3 on v2

--- a/solution.py
+++ b/solution.py
@@ -10,6 +10,7 @@
 N_LAT = 8
 DIRECT = 8
 EXTRA = 8
+PARTS = 4
 VMEM = pl.BlockSpec(memory_space=pltpu.VMEM)
 SMEM = pl.BlockSpec(memory_space=pltpu.SMEM)
 HBM = pl.BlockSpec(memory_space=pltpu.HBM)
@@ -133,11 +134,12 @@
 
 def copies_out(refs, held, semaphores):
     copies, at = [], 0
-    for k, ref in enumerate(refs):
-        rows = ref.shape[1] - EXTRA
-        copy = pltpu.make_async_copy(held.at[:, at : at + rows], ref.at[:, :rows], semaphores.at[k])
-        at += rows
-        copies.append((at, copy))
+    for ref in refs:
+        rows = (ref.shape[1] - EXTRA) // PARTS
+        for k in range(PARTS):
+            source, target = held.at[:, at : at + rows], ref.at[:, k * rows : (k + 1) * rows]
+            copies.append((at + rows, pltpu.make_async_copy(source, target, semaphores.at[len(copies)])))
+            at += rows
     return copies
 
 
@@ -182,9 +184,16 @@
     held, made, transmit, square, loads, stores = refs[:6]
     _, tiles, points, shots = held.shape
     copy_transmit = pltpu.make_async_copy(transmit_ref, transmit, loads.at[1])
-    copy_source = pltpu.make_async_copy(source_ref, held, loads.at[0])
+    share = tiles // PARTS
+    copies_source = [
+        pltpu.make_async_copy(
+            source_ref.at[:, k * share : (k + 1) * share], held.at[:, k * share : (k + 1) * share], loads.at[2 + k]
+        )
+        for k in range(PARTS)
+    ]
     copy_transmit.start()
-    copy_source.start()
+    for copy in copies_source:
+        copy.start()
     outgoing = copies_out(sent_refs, made, stores)
     copy_transmit.wait()
     columns_of(transmit[...], square)
@@ -195,15 +204,16 @@
             beside[part, :, :tiles] = square[:points, part * tiles : (part + 1) * tiles]
         pack = pltpu.make_async_copy(beside, packed_ref, pack_stores.at[0])
         pack.start()
-    copy_source.wait()
     start_field = jnp.zeros((points, shots), jnp.float32)
     for t in range(tiles):
+        if t % share == 0:
+            copies_source[t // share].wait()
         rows = slice(t * points, (t + 1) * points)
         made[0, rows], made[1, rows] = transmitted(
             (held[0, t], held[1, t]), wide(square, t, tiles, points, shots), (start_field, start_field)
         )
         for ready, copy in outgoing:
-            if ready == rows.stop:
+            if rows.start < ready <= rows.stop:
                 copy.start()
     if packs:
         pack.wait()
@@ -218,8 +228,8 @@
         field_scratch(source),
         flat_scratch(source),
         *transmit_scratch(source),
-        pltpu.SemaphoreType.DMA((2,)),
-        pltpu.SemaphoreType.DMA((len(counts),)),
+        pltpu.SemaphoreType.DMA((2 + PARTS,)),
+        pltpu.SemaphoreType.DMA((PARTS * len(counts),)),
     ]
     if packs:
         shapes.append(jax.ShapeDtypeStruct((2, points, shots), jnp.float32))
@@ -299,30 +309,61 @@
     )(active, blocks, *map(in_hbm, values))
 
 
-def rest_kernel(first, near_pieces, far_pieces, counts, active_ref, blocks_ref, partial_ref, *refs):
+def far_kernel(pieces, active_ref, blocks_ref, partial_ref, *refs):
+    out_ref, held, high_ref, low_ref, loads = refs[pieces:]
+    _, tiles, points, shots = out_ref.shape
+
+    @pl.when(active_ref[0] > 0)
+    def _():
+        copies = copies_in(refs[:pieces], held, loads)
+        for copy in copies:
+            copy.start()
+        clear_ends(high_ref, low_ref, points)
+        for copy in copies:
+            copy.wait()
+        for t in range(tiles):
+            rows = slice(t * points, (t + 1) * points)
+            convert((held[0, rows], held[1, rows]), high_ref, low_ref, t)
+        for t in range(tiles):
+            four = product(blocks_ref[t, 2], high_ref, low_ref, t, points)
+            real, imaginary = complex_parts(four, points, shots)
+            out_ref[0, t] = partial_ref[0, t] + real
+            out_ref[1, t] = partial_ref[1, t] + imaginary
+
+
+def far_sum(active, blocks, partial, far):
+    return pl.pallas_call(
+        functools.partial(far_kernel, len(far)),
+        in_specs=[SMEM, VMEM, VMEM] + [HBM] * len(far),
+        out_specs=VMEM,
+        out_shape=jax.ShapeDtypeStruct(partial.shape, jnp.float32),
+        scratch_shapes=[flat_scratch(partial), *split_scratch(partial), pltpu.SemaphoreType.DMA((len(far),))],
+        **params(1_000, 1_000),
+    )(active, blocks, partial, *map(in_hbm, far))
+
+
+def near_kernel(first, pieces, counts, active_ref, blocks_ref, partial_ref, *refs):
     if not first:
         refs = refs[1:]
     if counts:
         factor_ref, source_ref, refs = refs[0], refs[1], refs[2:]
-    near_refs, refs = refs[:near_pieces], refs[near_pieces:]
-    far_refs, refs = refs[:far_pieces], refs[far_pieces:]
+    near_refs, refs = refs[:pieces], refs[pieces:]
     out_ref, sent_refs, refs = refs[0], refs[1 : 1 + len(counts)], refs[1 + len(counts) :]
-    near, far, made, near_high, near_low, far_high, far_low, near_loads, far_loads, stores = refs[:10]
+    held, made, high_ref, low_ref, loads, stores = refs[:6]
     if counts:
-        factor, source, sent, more_loads, more_stores = refs[10:]
+        factor, source, sent, more_loads, more_stores = refs[6:]
     _, tiles, points, shots = out_ref.shape
 
     @pl.when(active_ref[0] > 0)
     def _():
-        copies = copies_in(near_refs, near, near_loads) + copies_in(far_refs, far, far_loads)
+        copies = copies_in(near_refs, held, loads)
         if counts:
             copies.append(pltpu.make_async_copy(factor_ref, factor, more_loads.at[0]))
             copies.append(pltpu.make_async_copy(source_ref, source, more_loads.at[1]))
             outgoing = copies_out(sent_refs, sent, more_stores)
         for copy in copies:
             copy.start()
-        clear_ends(near_high, near_low, points)
-        clear_ends(far_high, far_low, points)
+        clear_ends(high_ref, low_ref, points)
         for copy in copies:
             copy.wait()
         half = tiles // 2
@@ -332,11 +373,9 @@
         ]
         for t in range(tiles):
             rows = slice(t * points, (t + 1) * points)
-            convert((near[0, rows], near[1, rows]), near_high, near_low, t)
-            convert((far[0, rows], far[1, rows]), far_high, far_low, t)
-        for t in range(tiles):
-            four = product(blocks_ref[t, 1], near_high, near_low, t, points)
-            four += product(blocks_ref[t, 2], far_high, far_low, t, points)
+            convert((held[0, rows], held[1, rows]), high_ref, low_ref, t)
+        for t in range(tiles):
+            four = product(blocks_ref[t, 1], high_ref, low_ref, t, points)
             real, imaginary = complex_parts(four, points, shots)
             real += partial_ref[0, t]
             imaginary += partial_ref[1, t]
@@ -347,7 +386,7 @@
                 factors = [jnp.broadcast_to(factor[p, :, t : t + 1], (points, shots)) for p in range(2)]
                 sent[0, rows], sent[1, rows] = transmitted((source[0, t], source[1, t]), factors, (real, imaginary))
                 for ready, copy in outgoing:
-                    if ready == rows.stop:
+                    if rows.start < ready <= rows.stop:
                         copy.start()
             for ready, copy in results:
                 if ready == t + 1:
@@ -356,10 +395,10 @@
             copy.wait()
 
 
-def rest_sum(active, blocks, partial, before, below, near, far, counts):
+def near_sum(active, blocks, partial, before, below, near, counts):
     shapes = [jax.ShapeDtypeStruct(partial.shape, jnp.float32)] + pieces_like(partial, counts)
-    scratch = [flat_scratch(partial)] * 2 + [field_scratch(partial)] + split_scratch(partial) * 2
-    scratch += [pltpu.SemaphoreType.DMA((count,)) for count in (len(near), len(far), 2)]
+    scratch = [flat_scratch(partial), field_scratch(partial), *split_scratch(partial)]
+    scratch += [pltpu.SemaphoreType.DMA((len(near),)), pltpu.SemaphoreType.DMA((2,))]
     specs, values, aliases = [SMEM, VMEM, VMEM], [active, blocks, partial], {}
     if before is not None:
         specs += [HBM]
@@ -373,17 +412,17 @@
             field_scratch(partial),
             flat_scratch(partial),
             pltpu.SemaphoreType.DMA((2,)),
-            pltpu.SemaphoreType.DMA((len(counts),)),
+            pltpu.SemaphoreType.DMA((PARTS * len(counts),)),
         ]
     return pl.pallas_call(
-        functools.partial(rest_kernel, before is None, len(near), len(far), counts),
-        in_specs=specs + [HBM] * (len(near) + len(far)),
+        functools.partial(near_kernel, before is None, len(near), counts),
+        in_specs=specs + [HBM] * len(near),
         out_specs=[HBM] * len(shapes),
         out_shape=shapes,
         scratch_shapes=scratch,
         input_output_aliases=aliases,
         **params(1_000_000_000, 4_000_000),
-    )(*values, *map(in_hbm, near + far))
+    )(*values, *map(in_hbm, near))
 
 
 def send(value, route):
@@ -426,7 +465,8 @@
         came = send(output, [(at(s, m), at(s, n)) for s in strips]) if n else None
         partial = own_sum(active, blocks, transmit, field, came)
         counts = () if n == levels - 1 else (tiles,)
-        output, *sent = rest_sum(active, blocks, partial, output, below, near, far, counts)
+        partial = far_sum(active, blocks, partial, far)
+        output, *sent = near_sum(active, blocks, partial, output, below, near, counts)
     return output[None]
 
 

time: 40.9 us -> 39.7 us (0.971)
  waiting for transfers between devices: 17.1 us -> 14.7 us
  Pallas kernels: 10.5 us -> 11.6 us
    ppermute x7, waiting for transfers between devices: 17.1 us -> 14.7 us  [send(): return lax.ppermute(value, 'depth', route)]
    pallas_call x2 -> x4, Pallas kernels: 3 us -> 4.08 us  [the longest x2 2.43 us: near_sum(): pl.pallas_call(functools.partial(near_kernel, before is None, len(near),...]
  transfers between devices with their start and end apart: 7 -> 7, of which waited for: 4 -> 4; matrix products, arithmetic and copies ran while one was open for 0% -> 0% of each run, Pallas kernels for 13% -> 18%
where the time goes in v3:
time: 39.7 us; the launch traced here: 39.1 us
  waiting for transfers between devices  14.7 us (37%)
  starting transfers between devices  12.7 us (32%)
  Pallas kernels  11.6 us (29%)
    ppermute x7, waiting for transfers between devices, send(): return lax.ppermute(value, 'depth', route)  14.7 us
    ppermute x7, starting transfers between devices, send(): return lax.ppermute(value, 'depth', route)  12.7 us
    pallas_call x1, Pallas kernels, arrange(): pl.pallas_call(arrange_kernel, in_specs=[SMEM, HBM, HBM], out_specs=VMEM,...  3.28 us
    pallas_call x2, Pallas kernels, near_sum(): pl.pallas_call(functools.partial(near_kernel, before is None, len(near),...  2.43 us
    pallas_call x1, Pallas kernels, first_field(): pl.pallas_call(functools.partial(first_kernel, counts, packs), in_specs=[...  2.12 us
    pallas_call x2, Pallas kernels, own_sum(): pl.pallas_call(functools.partial(own_kernel, came is None), in_specs=[SME...  2.08 us
    pallas_call x2, Pallas kernels, far_sum(): pl.pallas_call(functools.partial(far_kernel, len(far)), in_specs=[SMEM, V...  1.65 us
  transfers between devices with their start and end apart: 7, of which 4 were waited for; matrix products, arithmetic and copies ran while one was open for 0% of the time, Pallas kernels for 18%

profile of v3, /device:TPU:24, one launch (start us, length us, event | category | flops | bytes accessed | tf_op | source)
XLA Modules:
  0.0 39.1 jit_solution(2905056532001257680)
XLA Ops:
  0.0 2.1 %shard_map.46 = (f32[2,520,128]{2,1,0:T(8,128)}, f32[2,64,128]{2,1,0:T(8,128)S(1)}) custom-call(f32[2,8,64,128]{3,2,1,0:T(8,128)} %bitcast.5, f32[2,8,64]{2,1,0:T(8,128)} %transmit_ref.5), custom_call_target="tpu_custom_call" | custom-call | flops 500000000 | bytes 4000000 | tf_op jit(solution)/shard_map/pallas_call | solution.py:237
  2.1 1.5 %collective-permute-start = (f32[2,520,128]{2,1,0:T(8,128)}, f32[2,520,128]{2,1,0:T(8,128)}, u32[]{:S(2)}, u32[]{:S(2)}) collective-permute-start(f32[2,520,128]{2,1,0:T(8,128)} %get-tuple-element.17), channel_id=1, source_target_pairs={{3,5},{5,3},{7,9},{9,7},{11,13},{13,11},{19,21},{21,19},{23,25},{2... | collective-permute-start | bytes 1597448 | tf_op jit(solution)/shard_map/ppermute | solution.py:429
  3.6 1.4 %collective-permute-start.3 = (f32[2,520,128]{2,1,0:T(8,128)}, f32[2,520,128]{2,1,0:T(8,128)}, u32[]{:S(2)}, u32[]{:S(2)}) collective-permute-start(f32[2,520,128]{2,1,0:T(8,128)} %get-tuple-element.17), channel_id=1, source_target_pairs={{1,3},{3,1},{5,7},{7,5},{9,11},{11,9},{13,15},{15,13},{17,19},{19,... | collective-permute-start | bytes 1597448 | tf_op jit(solution)/shard_map/ppermute | solution.py:429
  5.1 3.3 %shard_map.47.blocks_ref = bf16[8,3,256,192]{3,2,1,0:T(8,128)(2,1)S(1)} custom-call(s32[1]{0:T(128)} %bitcast.1.strip_ref, s32[8,9]{1,0:T(8,128)} %neighbours_ref.1, f32[8,2,64,576]{3,2,1,0:T(8,128)} %block_ref), custom_call_target="tpu_custom_call" | custom-call | flops 4000000 | bytes 6000000 | tf_op jit(solution)/shard_map/pallas_call | solution.py:75
  8.4 4.6 %collective-permute-start.2 = (f32[2,8,64,128]{3,2,1,0:T(8,128)}, f32[2,8,64,128]{3,2,1,0:T(8,128)}, u32[]{:S(2)}, u32[]{:S(2)}) collective-permute-start(f32[2,8,64,128]{3,2,1,0:T(8,128)} %bitcast.6), channel_id=1, source_target_pairs={{0,1},{2,3},{4,5},{6,7},{8,9},{10,11},{12,13},{14,15},{16,17},{18,... | collective-permute-start | bytes 1572872 | tf_op jit(solution)/shard_map/ppermute | solution.py:429
  12.9 1.3 %collective-permute-start.1 = (f32[2,64,128]{2,1,0:T(8,128)S(1)}, f32[2,64,128]{2,1,0:T(8,128)S(1)}, u32[]{:S(2)}, u32[]{:S(2)}) collective-permute-start(f32[2,64,128]{2,1,0:T(8,128)S(1)} %get-tuple-element.19), channel_id=1, source_target_pairs={{0,1},{2,3},{4,5},{6,7},{8,9},{10,11},{12,13},{14,15},{16,17},{18,... | collective-permute-start | bytes 196616 | tf_op jit(solution)/shard_map/ppermute | solution.py:429
  14.3 0.0 collective-permute-done.refs_0_
  14.3 0.8 %collective-permute-done.1.refs_0_ = f32[2,64,128]{2,1,0:T(8,128)S(1)} collective-permute-done((f32[2,64,128]{2,1,0:T(8,128)S(1)}, f32[2,64,128]{2,1,0:T(8,128)S(1)}, u32[]{:S(2)}, u32[]{:S(2)}) %collective-permute-start.1) | collective-permute-done | bytes 65568 | tf_op jit(solution)/shard_map/ppermute | solution.py:429
  15.1 0.0 collective-permute-done.2.refs_1_
  15.1 0.0 collective-permute-done.3.refs_2_
  15.1 0.1 shard_map.50
  15.2 1.3 %collective-permute-start.5 = (f32[2,520,128]{2,1,0:T(8,128)}, f32[2,520,128]{2,1,0:T(8,128)}, u32[]{:S(2)}, u32[]{:S(2)}) collective-permute-start(f32[2,520,128]{2,1,0:T(8,128)} %get-tuple-element.22), channel_id=1, source_target_pairs={{3,4},{5,2},{7,8},{9,6},{11,12},{13,10},{19,20},{21,18},{23,24},{2... | collective-permute-start | bytes 1597448 | tf_op jit(solution)/shard_map/ppermute | solution.py:429
  16.5 1.3 %collective-permute-start.6 = (f32[2,520,128]{2,1,0:T(8,128)}, f32[2,520,128]{2,1,0:T(8,128)}, u32[]{:S(2)}, u32[]{:S(2)}) collective-permute-start(f32[2,520,128]{2,1,0:T(8,128)} %get-tuple-element.22), channel_id=1, source_target_pairs={{1,2},{3,0},{5,6},{7,4},{9,10},{11,8},{13,14},{15,12},{17,18},{19,... | collective-permute-start | bytes 1597448 | tf_op jit(solution)/shard_map/ppermute | solution.py:429
  17.8 1.3 %collective-permute-start.4 = (f32[2,8,64,128]{3,2,1,0:T(8,128)}, f32[2,8,64,128]{3,2,1,0:T(8,128)}, u32[]{:S(2)}, u32[]{:S(2)}) collective-permute-start(f32[2,8,64,128]{3,2,1,0:T(8,128)} %get-tuple-element.21.refs_0_), channel_id=1, source_target_pairs={{1,0},{3,2},{5,4},{7,6},{9,8},{11,10},{13,12},{15,14},{17,16},{19,... | collective-permute-start | bytes 1572872 | tf_op jit(solution)/shard_map/ppermute | solution.py:429
  19.1 9.7 %collective-permute-done.4.refs_0_ = f32[2,8,64,128]{3,2,1,0:T(8,128)} collective-permute-done((f32[2,8,64,128]{3,2,1,0:T(8,128)}, f32[2,8,64,128]{3,2,1,0:T(8,128)}, u32[]{:S(2)}, u32[]{:S(2)}) %collective-permute-start.4) | collective-permute-done | bytes 524320 | tf_op jit(solution)/shard_map/ppermute | solution.py:429
  28.8 2.0 %shard_map.51.partial_ref = f32[2,8,64,128]{3,2,1,0:T(8,128)S(1)} custom-call(s32[1]{0:T(128)} %bitcast.active_ref, bf16[8,3,256,192]{3,2,1,0:T(8,128)(2,1)S(1)} %shard_map.47.blocks_ref, f32[2,8,64]{2,1,0:T(8,128)} %transmit_ref.5, f32[2,8,64,128]{3,2,1,0:T(8,128)} %bitcast.8, f32[2,8,64,128]{3,2,1,0:T(8,128)} %collective-permute-done.4.refs_0_), custom_call_target="tpu_custom_call" | custom-call | flops 1000 | bytes 1000 | tf_op jit(solution)/shard_map/pallas_call | solution.py:296
  30.8 0.4 collective-permute-done.5.refs_0_
  31.2 1.6 %shard_map.52.partial_ref = f32[2,8,64,128]{3,2,1,0:T(8,128)S(1)} custom-call(s32[1]{0:T(128)} %bitcast.active_ref, bf16[8,3,256,192]{3,2,1,0:T(8,128)(2,1)S(1)} %shard_map.47.blocks_ref, f32[2,8,64,128]{3,2,1,0:T(8,128)S(1)} %shard_map.51.partial_ref, f32[2,520,128]{2,1,0:T(8,128)} %collective-permute-done.5.refs_0_), custom_call_target="tpu_custom_call" | custom-call | flops 1000 | bytes 1000 | tf_op jit(solution)/shard_map/pallas_call | solution.py:335
  32.8 3.9 %collective-permute-done.6.refs_1_ = f32[2,520,128]{2,1,0:T(8,128)} collective-permute-done((f32[2,520,128]{2,1,0:T(8,128)}, f32[2,520,128]{2,1,0:T(8,128)}, u32[]{:S(2)}, u32[]{:S(2)}) %collective-permute-start.6) | collective-permute-done | bytes 532512 | tf_op jit(solution)/shard_map/ppermute | solution.py:429
  36.7 2.3 %shard_map.53 = f32[2,8,64,128]{3,2,1,0:T(8,128)} custom-call(s32[1]{0:T(128)} %bitcast.active_ref, bf16[8,3,256,192]{3,2,1,0:T(8,128)(2,1)S(1)} %shard_map.47.blocks_ref, f32[2,8,64,128]{3,2,1,0:T(8,128)S(1)} %shard_map.52.partial_ref, f32[2,8,64,128]{3,2,1,0:T(8,128)} %get-tuple-element.21.refs_0_, ...), custom_call_target="tpu_custom_call", output_to_operand_aliasing={{}: (3, {})} | custom-call | flops 1000000000 | bytes 4000000 | tf_op jit(solution)/shard_map/pallas_call | solution.py:417
  (2 shorter events, 0.1 us)
Async XLA Ops:
  2.1 12.1 %collective-permute-start = (f32[2,520,128]{2,1,0:T(8,128)}, f32[2,520,128]{2,1,0:T(8,128)}, u32[]{:S(2)}, u32[]{:S(2)}) collective-permute-start(f32[2,520,128]{2,1,0:T(8,128)} %get-tuple-element.17), channel_id=1, source_target_pairs={{3,5},{5,3},{7,9},{9,7},{11,13},{13,11},{19,21},{21,19},{23,25},{2... | collective-permute-start | bytes 1597448 | tf_op jit(solution)/shard_map/ppermute | solution.py:429
  3.6 11.5 %collective-permute-start.3 = (f32[2,520,128]{2,1,0:T(8,128)}, f32[2,520,128]{2,1,0:T(8,128)}, u32[]{:S(2)}, u32[]{:S(2)}) collective-permute-start(f32[2,520,128]{2,1,0:T(8,128)} %get-tuple-element.17), channel_id=1, source_target_pairs={{1,3},{3,1},{5,7},{7,5},{9,11},{11,9},{13,15},{15,13},{17,19},{19,... | collective-permute-start | bytes 1597448 | tf_op jit(solution)/shard_map/ppermute | solution.py:429
  8.4 6.7 %collective-permute-start.2 = (f32[2,8,64,128]{3,2,1,0:T(8,128)}, f32[2,8,64,128]{3,2,1,0:T(8,128)}, u32[]{:S(2)}, u32[]{:S(2)}) collective-permute-start(f32[2,8,64,128]{3,2,1,0:T(8,128)} %bitcast.6), channel_id=1, source_target_pairs={{0,1},{2,3},{4,5},{6,7},{8,9},{10,11},{12,13},{14,15},{16,17},{18,... | collective-permute-start | bytes 1572872 | tf_op jit(solution)/shard_map/ppermute | solution.py:429
  12.9 2.2 %collective-permute-start.1 = (f32[2,64,128]{2,1,0:T(8,128)S(1)}, f32[2,64,128]{2,1,0:T(8,128)S(1)}, u32[]{:S(2)}, u32[]{:S(2)}) collective-permute-start(f32[2,64,128]{2,1,0:T(8,128)S(1)} %get-tuple-element.19), channel_id=1, source_target_pairs={{0,1},{2,3},{4,5},{6,7},{8,9},{10,11},{12,13},{14,15},{16,17},{18,... | collective-permute-start | bytes 196616 | tf_op jit(solution)/shard_map/ppermute | solution.py:429
  15.2 16.0 %collective-permute-start.5 = (f32[2,520,128]{2,1,0:T(8,128)}, f32[2,520,128]{2,1,0:T(8,128)}, u32[]{:S(2)}, u32[]{:S(2)}) collective-permute-start(f32[2,520,128]{2,1,0:T(8,128)} %get-tuple-element.22), channel_id=1, source_target_pairs={{3,4},{5,2},{7,8},{9,6},{11,12},{13,10},{19,20},{21,18},{23,24},{2... | collective-permute-start | bytes 1597448 | tf_op jit(solution)/shard_map/ppermute | solution.py:429
  16.5 20.2 %collective-permute-start.6 = (f32[2,520,128]{2,1,0:T(8,128)}, f32[2,520,128]{2,1,0:T(8,128)}, u32[]{:S(2)}, u32[]{:S(2)}) collective-permute-start(f32[2,520,128]{2,1,0:T(8,128)} %get-tuple-element.22), channel_id=1, source_target_pairs={{1,2},{3,0},{5,6},{7,4},{9,10},{11,8},{13,14},{15,12},{17,18},{19,... | collective-permute-start | bytes 1597448 | tf_op jit(solution)/shard_map/ppermute | solution.py:429
  17.8 11.0 %collective-permute-start.4 = (f32[2,8,64,128]{3,2,1,0:T(8,128)}, f32[2,8,64,128]{3,2,1,0:T(8,128)}, u32[]{:S(2)}, u32[]{:S(2)}) collective-permute-start(f32[2,8,64,128]{3,2,1,0:T(8,128)} %get-tuple-element.21.refs_0_), channel_id=1, source_target_pairs={{1,0},{3,2},{5,4},{7,6},{9,8},{11,10},{13,12},{15,14},{17,16},{19,... | collective-permute-start | bytes 1572872 | tf_op jit(solution)/shard_map/ppermute | solution.py:429

commit v4 on v3

--- a/solution.py
+++ b/solution.py
@@ -8,13 +8,12 @@
 from jax.sharding import PartitionSpec as P
 
 N_LAT = 8
-DIRECT = 8
 EXTRA = 8
-PARTS = 4
+PARTS = 2
 VMEM = pl.BlockSpec(memory_space=pltpu.VMEM)
 SMEM = pl.BlockSpec(memory_space=pltpu.SMEM)
 HBM = pl.BlockSpec(memory_space=pltpu.HBM)
-LIMIT = 24 * 1024 * 1024
+LIMIT = 16 * 1024 * 1024
 
 
 def split(value):
@@ -123,23 +122,16 @@
     return real, imaginary
 
 
-def copies_in(refs, held, semaphores):
-    copies, at = [], 0
-    for k, ref in enumerate(refs):
-        rows = ref.shape[1] - EXTRA
-        copies.append(pltpu.make_async_copy(ref.at[:, :rows], held.at[:, at : at + rows], semaphores.at[k]))
-        at += rows
-    return copies
-
-
-def copies_out(refs, held, semaphores):
-    copies, at = [], 0
-    for ref in refs:
-        rows = (ref.shape[1] - EXTRA) // PARTS
-        for k in range(PARTS):
-            source, target = held.at[:, at : at + rows], ref.at[:, k * rows : (k + 1) * rows]
-            copies.append((at + rows, pltpu.make_async_copy(source, target, semaphores.at[len(copies)])))
-            at += rows
+def copy_in(ref, held, semaphore):
+    return pltpu.make_async_copy(ref.at[:, : held.shape[1]], held, semaphore)
+
+
+def copies_out(ref, held, semaphores):
+    rows = held.shape[1] // PARTS
+    copies = []
+    for k in range(PARTS):
+        part = slice(k * rows, (k + 1) * rows)
+        copies.append((part.stop, pltpu.make_async_copy(held.at[:, part], ref.at[:, part], semaphores.at[k])))
     return copies
 
 
@@ -154,9 +146,9 @@
     )
 
 
-def pieces_like(field, counts):
-    _, _, points, shots = field.shape
-    return [jax.ShapeDtypeStruct((2, count * points + EXTRA, shots), jnp.float32) for count in counts]
+def sent_shape(field, extra):
+    _, tiles, points, shots = field.shape
+    return jax.ShapeDtypeStruct((2, tiles * points + extra, shots), jnp.float32)
 
 
 def field_scratch(field):
@@ -177,10 +169,9 @@
     return [pltpu.VMEM((2, *field.shape[1:3]), jnp.float32), pltpu.VMEM((128, 128), jnp.float32)]
 
 
-def first_kernel(counts, packs, source_ref, transmit_ref, *refs):
-    sent_refs, refs = refs[: len(counts)], refs[len(counts) :]
+def first_kernel(packs, source_ref, transmit_ref, sent_ref, *refs):
     if packs:
-        packed_ref, refs = refs[0], refs[1:]
+        factor_ref, refs = refs[0], refs[1:]
     held, made, transmit, square, loads, stores = refs[:6]
     _, tiles, points, shots = held.shape
     copy_transmit = pltpu.make_async_copy(transmit_ref, transmit, loads.at[1])
@@ -194,7 +185,7 @@
     copy_transmit.start()
     for copy in copies_source:
         copy.start()
-    outgoing = copies_out(sent_refs, made, stores)
+    outgoing = copies_out(sent_ref, made, stores)
     copy_transmit.wait()
     columns_of(transmit[...], square)
     if packs:
@@ -202,7 +193,7 @@
         beside[...] = jnp.zeros_like(beside)
         for part in range(2):
             beside[part, :, :tiles] = square[:points, part * tiles : (part + 1) * tiles]
-        pack = pltpu.make_async_copy(beside, packed_ref, pack_stores.at[0])
+        pack = pltpu.make_async_copy(beside, factor_ref, pack_stores.at[0])
         pack.start()
     start_field = jnp.zeros((points, shots), jnp.float32)
     for t in range(tiles):
@@ -221,21 +212,21 @@
         copy.wait()
 
 
-def first_field(source, transmit, counts, packs):
+def first_field(source, transmit, packs):
     _, _, points, shots = source.shape
-    shapes = pieces_like(source, counts)
+    shapes = [sent_shape(source, 0)]
     scratch = [
         field_scratch(source),
         flat_scratch(source),
         *transmit_scratch(source),
         pltpu.SemaphoreType.DMA((2 + PARTS,)),
-        pltpu.SemaphoreType.DMA((PARTS * len(counts),)),
+        pltpu.SemaphoreType.DMA((PARTS,)),
     ]
     if packs:
         shapes.append(jax.ShapeDtypeStruct((2, points, shots), jnp.float32))
         scratch += [pltpu.VMEM((2, points, shots), jnp.float32), pltpu.SemaphoreType.DMA((1,))]
     return pl.pallas_call(
-        functools.partial(first_kernel, counts, packs),
+        functools.partial(first_kernel, packs),
         in_specs=[HBM, HBM],
         out_specs=[HBM] * len(shapes),
         out_shape=shapes,
@@ -309,18 +300,15 @@
     )(active, blocks, *map(in_hbm, values))
 
 
-def far_kernel(pieces, active_ref, blocks_ref, partial_ref, *refs):
-    out_ref, held, high_ref, low_ref, loads = refs[pieces:]
+def far_kernel(active_ref, blocks_ref, partial_ref, far_ref, out_ref, held, high_ref, low_ref, loads):
     _, tiles, points, shots = out_ref.shape
 
     @pl.when(active_ref[0] > 0)
     def _():
-        copies = copies_in(refs[:pieces], held, loads)
-        for copy in copies:
-            copy.start()
+        copy = copy_in(far_ref, held, loads.at[0])
+        copy.start()
         clear_ends(high_ref, low_ref, points)
-        for copy in copies:
-            copy.wait()
+        copy.wait()
         for t in range(tiles):
             rows = slice(t * points, (t + 1) * points)
             convert((held[0, rows], held[1, rows]), high_ref, low_ref, t)
@@ -333,34 +321,35 @@
 
 def far_sum(active, blocks, partial, far):
     return pl.pallas_call(
-        functools.partial(far_kernel, len(far)),
-        in_specs=[SMEM, VMEM, VMEM] + [HBM] * len(far),
+        far_kernel,
+        in_specs=[SMEM, VMEM, VMEM, HBM],
         out_specs=VMEM,
         out_shape=jax.ShapeDtypeStruct(partial.shape, jnp.float32),
-        scratch_shapes=[flat_scratch(partial), *split_scratch(partial), pltpu.SemaphoreType.DMA((len(far),))],
+        scratch_shapes=[flat_scratch(partial), *split_scratch(partial), pltpu.SemaphoreType.DMA((1,))],
         **params(1_000, 1_000),
-    )(active, blocks, partial, *map(in_hbm, far))
-
-
-def near_kernel(first, pieces, counts, active_ref, blocks_ref, partial_ref, *refs):
+    )(active, blocks, partial, in_hbm(far))
+
+
+def near_kernel(first, sends, active_ref, blocks_ref, partial_ref, *refs):
     if not first:
         refs = refs[1:]
-    if counts:
+    if sends:
         factor_ref, source_ref, refs = refs[0], refs[1], refs[2:]
-    near_refs, refs = refs[:pieces], refs[pieces:]
-    out_ref, sent_refs, refs = refs[0], refs[1 : 1 + len(counts)], refs[1 + len(counts) :]
+    near_ref, out_ref, refs = refs[0], refs[1], refs[2:]
+    if sends:
+        sent_ref, refs = refs[0], refs[1:]
     held, made, high_ref, low_ref, loads, stores = refs[:6]
-    if counts:
+    if sends:
         factor, source, sent, more_loads, more_stores = refs[6:]
     _, tiles, points, shots = out_ref.shape
 
     @pl.when(active_ref[0] > 0)
     def _():
-        copies = copies_in(near_refs, held, loads)
-        if counts:
+        copies = [copy_in(near_ref, held, loads.at[0])]
+        if sends:
             copies.append(pltpu.make_async_copy(factor_ref, factor, more_loads.at[0]))
             copies.append(pltpu.make_async_copy(source_ref, source, more_loads.at[1]))
-            outgoing = copies_out(sent_refs, sent, more_stores)
+            outgoing = copies_out(sent_ref, sent, more_stores)
         for copy in copies:
             copy.start()
         clear_ends(high_ref, low_ref, points)
@@ -381,7 +370,7 @@
             imaginary += partial_ref[1, t]
             made[0, t] = real
             made[1, t] = imaginary
-            if counts:
+            if sends:
                 rows = slice(t * points, (t + 1) * points)
                 factors = [jnp.broadcast_to(factor[p, :, t : t + 1], (points, shots)) for p in range(2)]
                 sent[0, rows], sent[1, rows] = transmitted((source[0, t], source[1, t]), factors, (real, imaginary))
@@ -391,20 +380,21 @@
             for ready, copy in results:
                 if ready == t + 1:
                     copy.start()
-        for _, copy in results + (outgoing if counts else []):
+        for _, copy in results + (outgoing if sends else []):
             copy.wait()
 
 
-def near_sum(active, blocks, partial, before, below, near, counts):
-    shapes = [jax.ShapeDtypeStruct(partial.shape, jnp.float32)] + pieces_like(partial, counts)
+def near_sum(active, blocks, partial, before, below, near):
+    sends = below is not None
+    shapes = [jax.ShapeDtypeStruct(partial.shape, jnp.float32)] + [sent_shape(partial, EXTRA)] * sends
     scratch = [flat_scratch(partial), field_scratch(partial), *split_scratch(partial)]
-    scratch += [pltpu.SemaphoreType.DMA((len(near),)), pltpu.SemaphoreType.DMA((2,))]
+    scratch += [pltpu.SemaphoreType.DMA((1,)), pltpu.SemaphoreType.DMA((2,))]
     specs, values, aliases = [SMEM, VMEM, VMEM], [active, blocks, partial], {}
     if before is not None:
         specs += [HBM]
         values += [in_hbm(before)]
         aliases = {3: 0}
-    if counts:
+    if sends:
         specs += [pl.BlockSpec(memory_space=pl.ANY), HBM]
         values += [below[0], in_hbm(below[1])]
         scratch += [
@@ -412,17 +402,17 @@
             field_scratch(partial),
             flat_scratch(partial),
             pltpu.SemaphoreType.DMA((2,)),
-            pltpu.SemaphoreType.DMA((PARTS * len(counts),)),
+            pltpu.SemaphoreType.DMA((PARTS,)),
         ]
     return pl.pallas_call(
-        functools.partial(near_kernel, before is None, len(near), counts),
-        in_specs=specs + [HBM] * len(near),
+        functools.partial(near_kernel, before is None, sends),
+        in_specs=specs + [HBM],
         out_specs=[HBM] * len(shapes),
         out_shape=shapes,
         scratch_shapes=scratch,
         input_output_aliases=aliases,
         **params(1_000_000_000, 4_000_000),
-    )(*values, *map(in_hbm, near))
+    )(*values, in_hbm(near))
 
 
 def send(value, route):
@@ -431,13 +421,11 @@
 
 def body(source, transmit, neighbours, extrapolator):
     field = source[0]
-    tiles = field.shape[1]
     levels = lax.axis_size("depth") // N_LAT
     place = lax.axis_index("depth")
     strip = place // levels
     level = levels - 1 - place % levels
     strips = range(N_LAT)
-    pieces = (DIRECT, tiles - DIRECT) if DIRECT < tiles else (tiles,)
     more = levels > 1
 
     def at(s, n):
@@ -446,27 +434,24 @@
     def far_of(s):
         return s + 1 if s % 2 else s - 1
 
-    sent = first_field(field, transmit, pieces, more)
+    sent = first_field(field, transmit, more)
     (*sent,), extrapolator = lax.optimization_barrier((sent, extrapolator))
     blocks = arrange(strip[None], neighbours, extrapolator)
     below = None
     if more:
-        *below, _ = lax.optimization_barrier((sent.pop(), field, blocks))
+        *below, _ = lax.optimization_barrier((sent[1], field, blocks))
         below = [send(b, [(p, p + 1) for p in range(N_LAT * levels) if (p + 1) % levels]) for b in below]
     output = None
     for n in range(levels):
         m = max(n - 1, 0)
         active = (level == n).astype(jnp.int32)[None]
         with_far = [s for s in strips if far_of(s) in strips]
-        near = [send(piece, [(at(s, m), at(s ^ 1, n)) for s in strips]) for piece in sent[::-1]][::-1]
-        far = [send(sent[0], [(at(s, m), at(far_of(s), n)) for s in with_far])]
-        if len(sent) > 1:
-            far.append(send(near[1], [(at(s ^ 1, n), at(far_of(s), n)) for s in with_far]))
+        near = send(sent[0], [(at(s, m), at(s ^ 1, n)) for s in strips])
+        far = send(sent[0], [(at(s, m), at(far_of(s), n)) for s in with_far])
         came = send(output, [(at(s, m), at(s, n)) for s in strips]) if n else None
         partial = own_sum(active, blocks, transmit, field, came)
-        counts = () if n == levels - 1 else (tiles,)
         partial = far_sum(active, blocks, partial, far)
-        output, *sent = near_sum(active, blocks, partial, output, below, near, counts)
+        output, *sent = near_sum(active, blocks, partial, output, None if n == levels - 1 else below, near)
     return output[None]
 
 

time: 39.7 us -> 38.7 us (0.975)
  waiting for transfers between devices: 14.7 us -> 13.5 us
    ppermute x7, waiting for transfers between devices: 14.7 us -> 13.5 us  [send(): return lax.ppermute(value, 'depth', route)]
where the time goes in v4:
time: 38.7 us; the launch traced here: 37.9 us
  waiting for transfers between devices  13.5 us (35%)
  starting transfers between devices  12.9 us (33%)
  Pallas kernels  11.4 us (29%)
    ppermute x7, waiting for transfers between devices, send(): return lax.ppermute(value, 'depth', route)  13.5 us
    ppermute x7, starting transfers between devices, send(): return lax.ppermute(value, 'depth', route)  12.9 us
    pallas_call x1, Pallas kernels, arrange(): pl.pallas_call(arrange_kernel, in_specs=[SMEM, HBM, HBM], out_specs=VMEM,...  3.27 us
    pallas_call x2, Pallas kernels, near_sum(): pl.pallas_call(functools.partial(near_kernel, before is None, sends), in_...  2.41 us
    pallas_call x2, Pallas kernels, own_sum(): pl.pallas_call(functools.partial(own_kernel, came is None), in_specs=[SME...  2.08 us
    pallas_call x1, Pallas kernels, first_field(): pl.pallas_call(functools.partial(first_kernel, packs), in_specs=[HBM, HBM...  2.03 us
    pallas_call x2, Pallas kernels, far_sum(): pl.pallas_call(far_kernel, in_specs=[SMEM, VMEM, VMEM, HBM], out_specs=VM...  1.65 us
  transfers between devices with their start and end apart: 7, of which 4 were waited for; matrix products, arithmetic and copies ran while one was open for 0% of the time, Pallas kernels for 18%

profile of v4, /device:TPU:24, one launch (start us, length us, event | category | flops | bytes accessed | tf_op | source)
XLA Modules:
  0.0 37.9 jit_solution(16724274913868681299)
XLA Ops:
  0.0 2.0 %shard_map.46 = (f32[2,512,128]{2,1,0:T(8,128)}, f32[2,64,128]{2,1,0:T(8,128)S(1)}) custom-call(f32[2,8,64,128]{3,2,1,0:T(8,128)} %bitcast.5, f32[2,8,64]{2,1,0:T(8,128)} %transmit_ref.5), custom_call_target="tpu_custom_call" | custom-call | flops 500000000 | bytes 4000000 | tf_op jit(solution)/shard_map/pallas_call | solution.py:228
  2.0 1.5 %collective-permute-start.3 = (f32[2,512,128]{2,1,0:T(8,128)}, f32[2,512,128]{2,1,0:T(8,128)}, u32[]{:S(2)}, u32[]{:S(2)}) collective-permute-start(f32[2,512,128]{2,1,0:T(8,128)} %get-tuple-element.17), channel_id=1, source_target_pairs={{1,3},{3,1},{5,7},{7,5},{9,11},{11,9},{13,15},{15,13},{17,19},{19,... | collective-permute-start | bytes 1572872 | tf_op jit(solution)/shard_map/ppermute | solution.py:419
  3.5 1.5 %collective-permute-start = (f32[2,512,128]{2,1,0:T(8,128)}, f32[2,512,128]{2,1,0:T(8,128)}, u32[]{:S(2)}, u32[]{:S(2)}) collective-permute-start(f32[2,512,128]{2,1,0:T(8,128)} %get-tuple-element.17), channel_id=1, source_target_pairs={{3,5},{5,3},{7,9},{9,7},{11,13},{13,11},{19,21},{21,19},{23,25},{2... | collective-permute-start | bytes 1572872 | tf_op jit(solution)/shard_map/ppermute | solution.py:419
  4.9 3.3 %shard_map.47.blocks_ref = bf16[8,3,256,192]{3,2,1,0:T(8,128)(2,1)S(1)} custom-call(s32[1]{0:T(128)} %bitcast.1.strip_ref, s32[8,9]{1,0:T(8,128)} %neighbours_ref.1, f32[8,2,64,576]{3,2,1,0:T(8,128)} %block_ref), custom_call_target="tpu_custom_call" | custom-call | flops 4000000 | bytes 6000000 | tf_op jit(solution)/shard_map/pallas_call | solution.py:74
  8.2 4.9 %collective-permute-start.2 = (f32[2,8,64,128]{3,2,1,0:T(8,128)}, f32[2,8,64,128]{3,2,1,0:T(8,128)}, u32[]{:S(2)}, u32[]{:S(2)}) collective-permute-start(f32[2,8,64,128]{3,2,1,0:T(8,128)} %bitcast.6), channel_id=1, source_target_pairs={{0,1},{2,3},{4,5},{6,7},{8,9},{10,11},{12,13},{14,15},{16,17},{18,... | collective-permute-start | bytes 1572872 | tf_op jit(solution)/shard_map/ppermute | solution.py:419
  13.1 1.3 %collective-permute-start.1 = (f32[2,64,128]{2,1,0:T(8,128)S(1)}, f32[2,64,128]{2,1,0:T(8,128)S(1)}, u32[]{:S(2)}, u32[]{:S(2)}) collective-permute-start(f32[2,64,128]{2,1,0:T(8,128)S(1)} %get-tuple-element.19), channel_id=1, source_target_pairs={{0,1},{2,3},{4,5},{6,7},{8,9},{10,11},{12,13},{14,15},{16,17},{18,... | collective-permute-start | bytes 196616 | tf_op jit(solution)/shard_map/ppermute | solution.py:419
  14.4 0.0 collective-permute-done.far_ref
  14.5 0.8 %collective-permute-done.1.refs_0_ = f32[2,64,128]{2,1,0:T(8,128)S(1)} collective-permute-done((f32[2,64,128]{2,1,0:T(8,128)S(1)}, f32[2,64,128]{2,1,0:T(8,128)S(1)}, u32[]{:S(2)}, u32[]{:S(2)}) %collective-permute-start.1) | collective-permute-done | bytes 65568 | tf_op jit(solution)/shard_map/ppermute | solution.py:419
  15.3 0.0 collective-permute-done.3.refs_2_
  15.3 0.0 collective-permute-done.2.refs_1_
  15.3 0.1 shard_map.50
  15.3 1.3 %collective-permute-start.5 = (f32[2,520,128]{2,1,0:T(8,128)}, f32[2,520,128]{2,1,0:T(8,128)}, u32[]{:S(2)}, u32[]{:S(2)}) collective-permute-start(f32[2,520,128]{2,1,0:T(8,128)} %get-tuple-element.22), channel_id=1, source_target_pairs={{3,4},{5,2},{7,8},{9,6},{11,12},{13,10},{19,20},{21,18},{23,24},{2... | collective-permute-start | bytes 1597448 | tf_op jit(solution)/shard_map/ppermute | solution.py:419
  16.6 1.3 %collective-permute-start.6 = (f32[2,520,128]{2,1,0:T(8,128)}, f32[2,520,128]{2,1,0:T(8,128)}, u32[]{:S(2)}, u32[]{:S(2)}) collective-permute-start(f32[2,520,128]{2,1,0:T(8,128)} %get-tuple-element.22), channel_id=1, source_target_pairs={{1,2},{3,0},{5,6},{7,4},{9,10},{11,8},{13,14},{15,12},{17,18},{19,... | collective-permute-start | bytes 1597448 | tf_op jit(solution)/shard_map/ppermute | solution.py:419
  17.9 1.3 %collective-permute-start.4 = (f32[2,8,64,128]{3,2,1,0:T(8,128)}, f32[2,8,64,128]{3,2,1,0:T(8,128)}, u32[]{:S(2)}, u32[]{:S(2)}) collective-permute-start(f32[2,8,64,128]{3,2,1,0:T(8,128)} %get-tuple-element.21.refs_0_), channel_id=1, source_target_pairs={{1,0},{3,2},{5,4},{7,6},{9,8},{11,10},{13,12},{15,14},{17,16},{19,... | collective-permute-start | bytes 1572872 | tf_op jit(solution)/shard_map/ppermute | solution.py:419
  19.3 8.6 %collective-permute-done.4.refs_0_ = f32[2,8,64,128]{3,2,1,0:T(8,128)} collective-permute-done((f32[2,8,64,128]{3,2,1,0:T(8,128)}, f32[2,8,64,128]{3,2,1,0:T(8,128)}, u32[]{:S(2)}, u32[]{:S(2)}) %collective-permute-start.4) | collective-permute-done | bytes 524320 | tf_op jit(solution)/shard_map/ppermute | solution.py:419
  27.8 2.0 %shard_map.51.partial_ref = f32[2,8,64,128]{3,2,1,0:T(8,128)S(1)} custom-call(s32[1]{0:T(128)} %bitcast.active_ref, bf16[8,3,256,192]{3,2,1,0:T(8,128)(2,1)S(1)} %shard_map.47.blocks_ref, f32[2,8,64]{2,1,0:T(8,128)} %transmit_ref.5, f32[2,8,64,128]{3,2,1,0:T(8,128)} %bitcast.8, f32[2,8,64,128]{3,2,1,0:T(8,128)} %collective-permute-done.4.refs_0_), custom_call_target="tpu_custom_call" | custom-call | flops 1000 | bytes 1000 | tf_op jit(solution)/shard_map/pallas_call | solution.py:287
  29.9 0.2 collective-permute-done.5.far_ref
  30.0 1.6 %shard_map.52.partial_ref = f32[2,8,64,128]{3,2,1,0:T(8,128)S(1)} custom-call(s32[1]{0:T(128)} %bitcast.active_ref, bf16[8,3,256,192]{3,2,1,0:T(8,128)(2,1)S(1)} %shard_map.47.blocks_ref, f32[2,8,64,128]{3,2,1,0:T(8,128)S(1)} %shard_map.51.partial_ref, f32[2,520,128]{2,1,0:T(8,128)} %collective-permute-done.5.far_ref), custom_call_target="tpu_custom_call" | custom-call | flops 1000 | bytes 1000 | tf_op jit(solution)/shard_map/pallas_call | solution.py:323
  31.7 3.9 %collective-permute-done.6.refs_1_ = f32[2,520,128]{2,1,0:T(8,128)} collective-permute-done((f32[2,520,128]{2,1,0:T(8,128)}, f32[2,520,128]{2,1,0:T(8,128)}, u32[]{:S(2)}, u32[]{:S(2)}) %collective-permute-start.6) | collective-permute-done | bytes 532512 | tf_op jit(solution)/shard_map/ppermute | solution.py:419
  35.6 2.3 %shard_map.53 = f32[2,8,64,128]{3,2,1,0:T(8,128)} custom-call(s32[1]{0:T(128)} %bitcast.active_ref, bf16[8,3,256,192]{3,2,1,0:T(8,128)(2,1)S(1)} %shard_map.47.blocks_ref, f32[2,8,64,128]{3,2,1,0:T(8,128)S(1)} %shard_map.52.partial_ref, f32[2,8,64,128]{3,2,1,0:T(8,128)} %get-tuple-element.21.refs_0_, ...), custom_call_target="tpu_custom_call", output_to_operand_aliasing={{}: (3, {})} | custom-call | flops 1000000000 | bytes 4000000 | tf_op jit(solution)/shard_map/pallas_call | solution.py:407
  (2 shorter events, 0.1 us)
Async XLA Ops:
  2.0 13.2 %collective-permute-start.3 = (f32[2,512,128]{2,1,0:T(8,128)}, f32[2,512,128]{2,1,0:T(8,128)}, u32[]{:S(2)}, u32[]{:S(2)}) collective-permute-start(f32[2,512,128]{2,1,0:T(8,128)} %get-tuple-element.17), channel_id=1, source_target_pairs={{1,3},{3,1},{5,7},{7,5},{9,11},{11,9},{13,15},{15,13},{17,19},{19,... | collective-permute-start | bytes 1572872 | tf_op jit(solution)/shard_map/ppermute | solution.py:419
  3.5 11.0 %collective-permute-start = (f32[2,512,128]{2,1,0:T(8,128)}, f32[2,512,128]{2,1,0:T(8,128)}, u32[]{:S(2)}, u32[]{:S(2)}) collective-permute-start(f32[2,512,128]{2,1,0:T(8,128)} %get-tuple-element.17), channel_id=1, source_target_pairs={{3,5},{5,3},{7,9},{9,7},{11,13},{13,11},{19,21},{21,19},{23,25},{2... | collective-permute-start | bytes 1572872 | tf_op jit(solution)/shard_map/ppermute | solution.py:419
  8.2 7.0 %collective-permute-start.2 = (f32[2,8,64,128]{3,2,1,0:T(8,128)}, f32[2,8,64,128]{3,2,1,0:T(8,128)}, u32[]{:S(2)}, u32[]{:S(2)}) collective-permute-start(f32[2,8,64,128]{3,2,1,0:T(8,128)} %bitcast.6), channel_id=1, source_target_pairs={{0,1},{2,3},{4,5},{6,7},{8,9},{10,11},{12,13},{14,15},{16,17},{18,... | collective-permute-start | bytes 1572872 | tf_op jit(solution)/shard_map/ppermute | solution.py:419
  13.1 2.2 %collective-permute-start.1 = (f32[2,64,128]{2,1,0:T(8,128)S(1)}, f32[2,64,128]{2,1,0:T(8,128)S(1)}, u32[]{:S(2)}, u32[]{:S(2)}) collective-permute-start(f32[2,64,128]{2,1,0:T(8,128)S(1)} %get-tuple-element.19), channel_id=1, source_target_pairs={{0,1},{2,3},{4,5},{6,7},{8,9},{10,11},{12,13},{14,15},{16,17},{18,... | collective-permute-start | bytes 196616 | tf_op jit(solution)/shard_map/ppermute | solution.py:419
  15.3 14.7 %collective-permute-start.5 = (f32[2,520,128]{2,1,0:T(8,128)}, f32[2,520,128]{2,1,0:T(8,128)}, u32[]{:S(2)}, u32[]{:S(2)}) collective-permute-start(f32[2,520,128]{2,1,0:T(8,128)} %get-tuple-element.22), channel_id=1, source_target_pairs={{3,4},{5,2},{7,8},{9,6},{11,12},{13,10},{19,20},{21,18},{23,24},{2... | collective-permute-start | bytes 1597448 | tf_op jit(solution)/shard_map/ppermute | solution.py:419
  16.6 19.0 %collective-permute-start.6 = (f32[2,520,128]{2,1,0:T(8,128)}, f32[2,520,128]{2,1,0:T(8,128)}, u32[]{:S(2)}, u32[]{:S(2)}) collective-permute-start(f32[2,520,128]{2,1,0:T(8,128)} %get-tuple-element.22), channel_id=1, source_target_pairs={{1,2},{3,0},{5,6},{7,4},{9,10},{11,8},{13,14},{15,12},{17,18},{19,... | collective-permute-start | bytes 1597448 | tf_op jit(solution)/shard_map/ppermute | solution.py:419
  17.9 9.9 %collective-permute-start.4 = (f32[2,8,64,128]{3,2,1,0:T(8,128)}, f32[2,8,64,128]{3,2,1,0:T(8,128)}, u32[]{:S(2)}, u32[]{:S(2)}) collective-permute-start(f32[2,8,64,128]{3,2,1,0:T(8,128)} %get-tuple-element.21.refs_0_), channel_id=1, source_target_pairs={{1,0},{3,2},{5,4},{7,6},{9,8},{11,10},{13,12},{15,14},{17,16},{19,... | collective-permute-start | bytes 1572872 | tf_op jit(solution)/shard_map/ppermute | solution.py:419

commit v5 on v4

--- a/solution.py
+++ b/solution.py
@@ -8,7 +8,6 @@
 from jax.sharding import PartitionSpec as P
 
 N_LAT = 8
-EXTRA = 8
 PARTS = 2
 VMEM = pl.BlockSpec(memory_space=pltpu.VMEM)
 SMEM = pl.BlockSpec(memory_space=pltpu.SMEM)
@@ -123,7 +122,7 @@
 
 
 def copy_in(ref, held, semaphore):
-    return pltpu.make_async_copy(ref.at[:, : held.shape[1]], held, semaphore)
+    return pltpu.make_async_copy(ref, held, semaphore)
 
 
 def copies_out(ref, held, semaphores):
@@ -146,9 +145,9 @@
     )
 
 
-def sent_shape(field, extra):
+def sent_shape(field):
     _, tiles, points, shots = field.shape
-    return jax.ShapeDtypeStruct((2, tiles * points + extra, shots), jnp.float32)
+    return jax.ShapeDtypeStruct((2, tiles * points, shots), jnp.float32)
 
 
 def field_scratch(field):
@@ -214,7 +213,7 @@
 
 def first_field(source, transmit, packs):
     _, _, points, shots = source.shape
-    shapes = [sent_shape(source, 0)]
+    shapes = [sent_shape(source)]
     scratch = [
         field_scratch(source),
         flat_scratch(source),
@@ -254,7 +253,7 @@
 
 def own_kernel(first, active_ref, blocks_ref, transmit_ref, source_ref, *refs):
     if not first:
-        came_ref, refs = refs[0], refs[1:]
+        came_ref, partial_ref, refs = refs[0], refs[1], refs[2:]
     out_ref, source, came, high_ref, low_ref, transmit, square, loads = refs
     _, tiles, points, shots = out_ref.shape
 
@@ -279,14 +278,16 @@
             convert(value, high_ref, low_ref, t)
         for t in range(tiles):
             four = product(blocks_ref[t, 0], high_ref, low_ref, t, points)
-            out_ref[0, t], out_ref[1, t] = complex_parts(four, points, shots)
-
-
-def own_sum(active, blocks, transmit, source, came):
+            real, imaginary = complex_parts(four, points, shots)
+            out_ref[0, t] = real if first else partial_ref[0, t] + real
+            out_ref[1, t] = imaginary if first else partial_ref[1, t] + imaginary
+
+
+def own_sum(active, blocks, transmit, source, came, partial):
     values = [transmit, source] if came is None else [transmit, source, came]
     return pl.pallas_call(
         functools.partial(own_kernel, came is None),
-        in_specs=[SMEM, VMEM] + [HBM] * len(values),
+        in_specs=[SMEM, VMEM] + [HBM] * len(values) + [VMEM] * (came is not None),
         out_specs=VMEM,
         out_shape=jax.ShapeDtypeStruct(source.shape, jnp.float32),
         scratch_shapes=[
@@ -297,10 +298,13 @@
             pltpu.SemaphoreType.DMA((3,)),
         ],
         **params(*((500_000_000, 2_000_000) if came is None else (1_000, 1_000))),
-    )(active, blocks, *map(in_hbm, values))
-
-
-def far_kernel(active_ref, blocks_ref, partial_ref, far_ref, out_ref, held, high_ref, low_ref, loads):
+    )(active, blocks, *map(in_hbm, values), *([] if came is None else [partial]))
+
+
+def far_kernel(adds, active_ref, blocks_ref, *refs):
+    if adds:
+        partial_ref, refs = refs[0], refs[1:]
+    far_ref, out_ref, held, high_ref, low_ref, loads = refs
     _, tiles, points, shots = out_ref.shape
 
     @pl.when(active_ref[0] > 0)
@@ -315,19 +319,20 @@
         for t in range(tiles):
             four = product(blocks_ref[t, 2], high_ref, low_ref, t, points)
             real, imaginary = complex_parts(four, points, shots)
-            out_ref[0, t] = partial_ref[0, t] + real
-            out_ref[1, t] = partial_ref[1, t] + imaginary
-
-
-def far_sum(active, blocks, partial, far):
+            out_ref[0, t] = partial_ref[0, t] + real if adds else real
+            out_ref[1, t] = partial_ref[1, t] + imaginary if adds else imaginary
+
+
+def far_sum(active, blocks, field, partial, far):
+    adds = partial is not None
     return pl.pallas_call(
-        far_kernel,
-        in_specs=[SMEM, VMEM, VMEM, HBM],
+        functools.partial(far_kernel, adds),
+        in_specs=[SMEM, VMEM] + [VMEM] * adds + [HBM],
         out_specs=VMEM,
-        out_shape=jax.ShapeDtypeStruct(partial.shape, jnp.float32),
-        scratch_shapes=[flat_scratch(partial), *split_scratch(partial), pltpu.SemaphoreType.DMA((1,))],
+        out_shape=jax.ShapeDtypeStruct(field.shape, jnp.float32),
+        scratch_shapes=[flat_scratch(field), *split_scratch(field), pltpu.SemaphoreType.DMA((1,))],
         **params(1_000, 1_000),
-    )(active, blocks, partial, in_hbm(far))
+    )(active, blocks, *([partial] if adds else []), in_hbm(far))
 
 
 def near_kernel(first, sends, active_ref, blocks_ref, partial_ref, *refs):
@@ -386,7 +391,7 @@
 
 def near_sum(active, blocks, partial, before, below, near):
     sends = below is not None
-    shapes = [jax.ShapeDtypeStruct(partial.shape, jnp.float32)] + [sent_shape(partial, EXTRA)] * sends
+    shapes = [jax.ShapeDtypeStruct(partial.shape, jnp.float32)] + [sent_shape(partial)] * sends
     scratch = [flat_scratch(partial), field_scratch(partial), *split_scratch(partial)]
     scratch += [pltpu.SemaphoreType.DMA((1,)), pltpu.SemaphoreType.DMA((2,))]
     specs, values, aliases = [SMEM, VMEM, VMEM], [active, blocks, partial], {}
@@ -449,8 +454,12 @@
         near = send(sent[0], [(at(s, m), at(s ^ 1, n)) for s in strips])
         far = send(sent[0], [(at(s, m), at(far_of(s), n)) for s in with_far])
         came = send(output, [(at(s, m), at(s, n)) for s in strips]) if n else None
-        partial = own_sum(active, blocks, transmit, field, came)
-        partial = far_sum(active, blocks, partial, far)
+        if n:
+            partial = far_sum(active, blocks, field, None, far)
+            partial = own_sum(active, blocks, transmit, field, came, partial)
+        else:
+            partial = own_sum(active, blocks, transmit, field, None, None)
+            partial = far_sum(active, blocks, field, partial, far)
         output, *sent = near_sum(active, blocks, partial, output, None if n == levels - 1 else below, near)
     return output[None]
 

time: 38.7 us -> 38.5 us (level)
  transfers between devices with their start and end apart: 7 -> 7, of which waited for: 4 -> 3; matrix products, arithmetic and copies ran while one was open for 0% -> 0% of each run, Pallas kernels for 18% -> 19%
where the time goes in v5:
time: 38.5 us; the launch traced here: 37.8 us
  waiting for transfers between devices  13.3 us (35%)
  starting transfers between devices  12.9 us (34%)
  Pallas kernels  11.4 us (30%)
    ppermute x7, waiting for transfers between devices, send(): return lax.ppermute(value, 'depth', route)  13.3 us
    ppermute x7, starting transfers between devices, send(): return lax.ppermute(value, 'depth', route)  12.9 us
    pallas_call x1, Pallas kernels, arrange(): pl.pallas_call(arrange_kernel, in_specs=[SMEM, HBM, HBM], out_specs=VMEM,...  3.28 us
    pallas_call x2, Pallas kernels, near_sum(): pl.pallas_call(functools.partial(near_kernel, before is None, sends), in_...  2.41 us
    pallas_call x2, Pallas kernels, own_sum(): pl.pallas_call(functools.partial(own_kernel, came is None), in_specs=[SME...  2.08 us
    pallas_call x1, Pallas kernels, first_field(): pl.pallas_call(functools.partial(first_kernel, packs), in_specs=[HBM, HBM...  2.03 us
    pallas_call x2, Pallas kernels, far_sum(): pl.pallas_call(functools.partial(far_kernel, adds), in_specs=[SMEM, VMEM]...  1.65 us
  transfers between devices with their start and end apart: 7, of which 3 were waited for; matrix products, arithmetic and copies ran while one was open for 0% of the time, Pallas kernels for 19%

profile of v5, /device:TPU:24, one launch (start us, length us, event | category | flops | bytes accessed | tf_op | source)
XLA Modules:
  0.0 37.8 jit_solution(14683414586395056863)
XLA Ops:
  0.0 2.0 %shard_map.46 = (f32[2,512,128]{2,1,0:T(8,128)}, f32[2,64,128]{2,1,0:T(8,128)S(1)}) custom-call(f32[2,8,64,128]{3,2,1,0:T(8,128)} %bitcast.5, f32[2,8,64]{2,1,0:T(8,128)} %transmit_ref.5), custom_call_target="tpu_custom_call" | custom-call | flops 500000000 | bytes 4000000 | tf_op jit(solution)/shard_map/pallas_call | solution.py:227
  2.0 1.5 %collective-permute-start.3 = (f32[2,512,128]{2,1,0:T(8,128)}, f32[2,512,128]{2,1,0:T(8,128)}, u32[]{:S(2)}, u32[]{:S(2)}) collective-permute-start(f32[2,512,128]{2,1,0:T(8,128)} %get-tuple-element.17), channel_id=1, source_target_pairs={{1,3},{3,1},{5,7},{7,5},{9,11},{11,9},{13,15},{15,13},{17,19},{19,... | collective-permute-start | bytes 1572872 | tf_op jit(solution)/shard_map/ppermute | solution.py:424
  3.5 1.5 %collective-permute-start = (f32[2,512,128]{2,1,0:T(8,128)}, f32[2,512,128]{2,1,0:T(8,128)}, u32[]{:S(2)}, u32[]{:S(2)}) collective-permute-start(f32[2,512,128]{2,1,0:T(8,128)} %get-tuple-element.17), channel_id=1, source_target_pairs={{3,5},{5,3},{7,9},{9,7},{11,13},{13,11},{19,21},{21,19},{23,25},{2... | collective-permute-start | bytes 1572872 | tf_op jit(solution)/shard_map/ppermute | solution.py:424
  5.0 3.3 %shard_map.47.blocks_ref = bf16[8,3,256,192]{3,2,1,0:T(8,128)(2,1)S(1)} custom-call(s32[1]{0:T(128)} %bitcast.1.strip_ref, s32[8,9]{1,0:T(8,128)} %neighbours_ref.1, f32[8,2,64,576]{3,2,1,0:T(8,128)} %block_ref), custom_call_target="tpu_custom_call" | custom-call | flops 4000000 | bytes 6000000 | tf_op jit(solution)/shard_map/pallas_call | solution.py:73
  8.3 4.8 %collective-permute-start.2 = (f32[2,8,64,128]{3,2,1,0:T(8,128)}, f32[2,8,64,128]{3,2,1,0:T(8,128)}, u32[]{:S(2)}, u32[]{:S(2)}) collective-permute-start(f32[2,8,64,128]{3,2,1,0:T(8,128)} %bitcast.6), channel_id=1, source_target_pairs={{0,1},{2,3},{4,5},{6,7},{8,9},{10,11},{12,13},{14,15},{16,17},{18,... | collective-permute-start | bytes 1572872 | tf_op jit(solution)/shard_map/ppermute | solution.py:424
  13.1 1.3 %collective-permute-start.1 = (f32[2,64,128]{2,1,0:T(8,128)S(1)}, f32[2,64,128]{2,1,0:T(8,128)S(1)}, u32[]{:S(2)}, u32[]{:S(2)}) collective-permute-start(f32[2,64,128]{2,1,0:T(8,128)S(1)} %get-tuple-element.19), channel_id=1, source_target_pairs={{0,1},{2,3},{4,5},{6,7},{8,9},{10,11},{12,13},{14,15},{16,17},{18,... | collective-permute-start | bytes 196616 | tf_op jit(solution)/shard_map/ppermute | solution.py:424
  14.4 0.0 collective-permute-done.refs_1_
  14.5 0.8 %collective-permute-done.1.refs_0_ = f32[2,64,128]{2,1,0:T(8,128)S(1)} collective-permute-done((f32[2,64,128]{2,1,0:T(8,128)S(1)}, f32[2,64,128]{2,1,0:T(8,128)S(1)}, u32[]{:S(2)}, u32[]{:S(2)}) %collective-permute-start.1) | collective-permute-done | bytes 65568 | tf_op jit(solution)/shard_map/ppermute | solution.py:424
  15.3 0.0 collective-permute-done.3.refs_2_
  15.3 0.0 collective-permute-done.2.refs_1_
  15.3 0.1 shard_map.50
  15.3 1.3 %collective-permute-start.5 = (f32[2,512,128]{2,1,0:T(8,128)}, f32[2,512,128]{2,1,0:T(8,128)}, u32[]{:S(2)}, u32[]{:S(2)}) collective-permute-start(f32[2,512,128]{2,1,0:T(8,128)} %get-tuple-element.22), channel_id=1, source_target_pairs={{3,4},{5,2},{7,8},{9,6},{11,12},{13,10},{19,20},{21,18},{23,24},{2... | collective-permute-start | bytes 1572872 | tf_op jit(solution)/shard_map/ppermute | solution.py:424
  16.6 1.3 %collective-permute-start.4 = (f32[2,8,64,128]{3,2,1,0:T(8,128)}, f32[2,8,64,128]{3,2,1,0:T(8,128)}, u32[]{:S(2)}, u32[]{:S(2)}) collective-permute-start(f32[2,8,64,128]{3,2,1,0:T(8,128)} %get-tuple-element.21.refs_0_), channel_id=1, source_target_pairs={{1,0},{3,2},{5,4},{7,6},{9,8},{11,10},{13,12},{15,14},{17,16},{19,... | collective-permute-start | bytes 1572872 | tf_op jit(solution)/shard_map/ppermute | solution.py:424
  17.9 1.3 %collective-permute-start.6 = (f32[2,512,128]{2,1,0:T(8,128)}, f32[2,512,128]{2,1,0:T(8,128)}, u32[]{:S(2)}, u32[]{:S(2)}) collective-permute-start(f32[2,512,128]{2,1,0:T(8,128)} %get-tuple-element.22), channel_id=1, source_target_pairs={{1,2},{3,0},{5,6},{7,4},{9,10},{11,8},{13,14},{15,12},{17,18},{19,... | collective-permute-start | bytes 1572872 | tf_op jit(solution)/shard_map/ppermute | solution.py:424
  19.2 10.7 %collective-permute-done.5.refs_0_ = f32[2,512,128]{2,1,0:T(8,128)} collective-permute-done((f32[2,512,128]{2,1,0:T(8,128)}, f32[2,512,128]{2,1,0:T(8,128)}, u32[]{:S(2)}, u32[]{:S(2)}) %collective-permute-start.5) | collective-permute-done | bytes 524320 | tf_op jit(solution)/shard_map/ppermute | solution.py:424
  29.9 1.6 %shard_map.51.refs_1_ = f32[2,8,64,128]{3,2,1,0:T(8,128)S(1)} custom-call(s32[1]{0:T(128)} %bitcast.active_ref, bf16[8,3,256,192]{3,2,1,0:T(8,128)(2,1)S(1)} %shard_map.47.blocks_ref, f32[2,512,128]{2,1,0:T(8,128)} %collective-permute-done.5.refs_0_), custom_call_target="tpu_custom_call" | custom-call | flops 1000 | bytes 1000 | tf_op jit(solution)/shard_map/pallas_call | solution.py:328
  31.6 0.0 collective-permute-done.4.refs_0_
  31.6 2.0 %shard_map.52.partial_ref = f32[2,8,64,128]{3,2,1,0:T(8,128)S(1)} custom-call(s32[1]{0:T(128)} %bitcast.active_ref, bf16[8,3,256,192]{3,2,1,0:T(8,128)(2,1)S(1)} %shard_map.47.blocks_ref, f32[2,8,64]{2,1,0:T(8,128)} %transmit_ref.5, f32[2,8,64,128]{3,2,1,0:T(8,128)} %bitcast.8, f32[2,8,64,128]{3,2,1,0:T(8,128)} %collective-permute-done.4.refs_0_, ...), custom_call_target="tpu_custom_call" | custom-call | flops 1000 | bytes 1000 | tf_op jit(solution)/shard_map/pallas_call | solution.py:288
  33.7 1.8 %collective-permute-done.6.refs_1_ = f32[2,512,128]{2,1,0:T(8,128)} collective-permute-done((f32[2,512,128]{2,1,0:T(8,128)}, f32[2,512,128]{2,1,0:T(8,128)}, u32[]{:S(2)}, u32[]{:S(2)}) %collective-permute-start.6) | collective-permute-done | bytes 524320 | tf_op jit(solution)/shard_map/ppermute | solution.py:424
  35.5 2.3 %shard_map.53 = f32[2,8,64,128]{3,2,1,0:T(8,128)} custom-call(s32[1]{0:T(128)} %bitcast.active_ref, bf16[8,3,256,192]{3,2,1,0:T(8,128)(2,1)S(1)} %shard_map.47.blocks_ref, f32[2,8,64,128]{3,2,1,0:T(8,128)S(1)} %shard_map.52.partial_ref, f32[2,8,64,128]{3,2,1,0:T(8,128)} %get-tuple-element.21.refs_0_, ...), custom_call_target="tpu_custom_call", output_to_operand_aliasing={{}: (3, {})} | custom-call | flops 1000000000 | bytes 4000000 | tf_op jit(solution)/shard_map/pallas_call | solution.py:412
  (2 shorter events, 0.1 us)
Async XLA Ops:
  2.0 13.2 %collective-permute-start.3 = (f32[2,512,128]{2,1,0:T(8,128)}, f32[2,512,128]{2,1,0:T(8,128)}, u32[]{:S(2)}, u32[]{:S(2)}) collective-permute-start(f32[2,512,128]{2,1,0:T(8,128)} %get-tuple-element.17), channel_id=1, source_target_pairs={{1,3},{3,1},{5,7},{7,5},{9,11},{11,9},{13,15},{15,13},{17,19},{19,... | collective-permute-start | bytes 1572872 | tf_op jit(solution)/shard_map/ppermute | solution.py:424
  3.5 10.9 %collective-permute-start = (f32[2,512,128]{2,1,0:T(8,128)}, f32[2,512,128]{2,1,0:T(8,128)}, u32[]{:S(2)}, u32[]{:S(2)}) collective-permute-start(f32[2,512,128]{2,1,0:T(8,128)} %get-tuple-element.17), channel_id=1, source_target_pairs={{3,5},{5,3},{7,9},{9,7},{11,13},{13,11},{19,21},{21,19},{23,25},{2... | collective-permute-start | bytes 1572872 | tf_op jit(solution)/shard_map/ppermute | solution.py:424
  8.3 7.0 %collective-permute-start.2 = (f32[2,8,64,128]{3,2,1,0:T(8,128)}, f32[2,8,64,128]{3,2,1,0:T(8,128)}, u32[]{:S(2)}, u32[]{:S(2)}) collective-permute-start(f32[2,8,64,128]{3,2,1,0:T(8,128)} %bitcast.6), channel_id=1, source_target_pairs={{0,1},{2,3},{4,5},{6,7},{8,9},{10,11},{12,13},{14,15},{16,17},{18,... | collective-permute-start | bytes 1572872 | tf_op jit(solution)/shard_map/ppermute | solution.py:424
  13.1 2.2 %collective-permute-start.1 = (f32[2,64,128]{2,1,0:T(8,128)S(1)}, f32[2,64,128]{2,1,0:T(8,128)S(1)}, u32[]{:S(2)}, u32[]{:S(2)}) collective-permute-start(f32[2,64,128]{2,1,0:T(8,128)S(1)} %get-tuple-element.19), channel_id=1, source_target_pairs={{0,1},{2,3},{4,5},{6,7},{8,9},{10,11},{12,13},{14,15},{16,17},{18,... | collective-permute-start | bytes 196616 | tf_op jit(solution)/shard_map/ppermute | solution.py:424
  15.3 14.6 %collective-permute-start.5 = (f32[2,512,128]{2,1,0:T(8,128)}, f32[2,512,128]{2,1,0:T(8,128)}, u32[]{:S(2)}, u32[]{:S(2)}) collective-permute-start(f32[2,512,128]{2,1,0:T(8,128)} %get-tuple-element.22), channel_id=1, source_target_pairs={{3,4},{5,2},{7,8},{9,6},{11,12},{13,10},{19,20},{21,18},{23,24},{2... | collective-permute-start | bytes 1572872 | tf_op jit(solution)/shard_map/ppermute | solution.py:424
  16.6 15.0 %collective-permute-start.4 = (f32[2,8,64,128]{3,2,1,0:T(8,128)}, f32[2,8,64,128]{3,2,1,0:T(8,128)}, u32[]{:S(2)}, u32[]{:S(2)}) collective-permute-start(f32[2,8,64,128]{3,2,1,0:T(8,128)} %get-tuple-element.21.refs_0_), channel_id=1, source_target_pairs={{1,0},{3,2},{5,4},{7,6},{9,8},{11,10},{13,12},{15,14},{17,16},{19,... | collective-permute-start | bytes 1572872 | tf_op jit(solution)/shard_map/ppermute | solution.py:424
  17.9 17.5 %collective-permute-start.6 = (f32[2,512,128]{2,1,0:T(8,128)}, f32[2,512,128]{2,1,0:T(8,128)}, u32[]{:S(2)}, u32[]{:S(2)}) collective-permute-start(f32[2,512,128]{2,1,0:T(8,128)} %get-tuple-element.22), channel_id=1, source_target_pairs={{1,2},{3,0},{5,6},{7,4},{9,10},{11,8},{13,14},{15,12},{17,18},{19,... | collective-permute-start | bytes 1572872 | tf_op jit(solution)/shard_map/ppermute | solution.py:424

commit v6 on v5

--- a/solution.py
+++ b/solution.py
@@ -32,31 +32,30 @@
     copy_index.wait()
     strip = strip_ref[0]
     near = 1 - 2 * lax.rem(strip, 2)
-    for t in range(tiles):
+    lane = lax.broadcasted_iota(jnp.int32, (points, width), 1)
+
+    def one_tile(t, carry):
         for k in range(9):
-            slot_of[t * 10 + k] = -1
+            slot_of[k] = 9
         for s in range(9):
             index = neighbours[t, s]
             safe = jnp.maximum(index, 0)
             offset = lax.div(safe, tiles) - strip
             column = lax.rem(safe, tiles) - t + 1
             group = jnp.where(offset == 0, 0, jnp.where(offset == near, 1, 2))
-            slot_of[t * 10 + jnp.where(index >= 0, group * 3 + column, 9)] = s
-    lane = lax.broadcasted_iota(jnp.int32, (points, width), 1)
-
-    def one_tile(t, carry):
+            slot_of[jnp.where(index >= 0, group * 3 + column, 9)] = s
         pltpu.make_async_copy(block_ref.at[t], held.at[t], loads.at[t]).wait()
         tail[:, :, :points] = held[t, :, :, 8 * points :]
+        tail[:, :, points:] = jnp.zeros_like(tail[:, :, points:])
         for group in range(3):
-            found = [slot_of[t * 10 + group * 3 + j] for j in range(3)]
-            safe = [jnp.maximum(s, 0) for s in found]
+            found = [slot_of[group * 3 + j] for j in range(3)]
             for part in range(2):
                 loaded = []
                 for j in range(3):
-                    start = pl.multiple_of(jnp.minimum(lax.div(safe[j], 2), 3) * width, width)
-                    value = jnp.where(safe[j] == 8, tail[part], held[t, part, :, pl.ds(start, width)])
-                    value = jnp.where(lax.rem(safe[j] + j, 2) == 0, value, pltpu.roll(value, points, 1))
-                    loaded.append(jnp.where(found[j] >= 0, value, 0.0))
+                    start = pl.multiple_of(jnp.minimum(found[j] >> 1, 3) * width, width)
+                    value = jnp.where(found[j] >= 8, tail[part], held[t, part, :, pl.ds(start, width)])
+                    value = jnp.where((found[j] + j) & 1 == 0, value, pltpu.roll(value, points, 1))
+                    loaded.append(value)
                 first = jnp.where(lane < points, loaded[0], loaded[1])
                 for at, value in ((0, first), (width, loaded[2][:, :points])):
                     high, low = split(value)
@@ -65,7 +64,7 @@
                     out_ref[t, group, (2 + part) * points : (3 + part) * points, columns] = low
         return carry
 
-    lax.fori_loop(0, tiles, one_tile, 0)
+    lax.fori_loop(0, tiles, one_tile, 0, unroll=True)
 
 
 def arrange(strip, neighbours, extrapolator):
@@ -79,7 +78,7 @@
             pltpu.SMEM(neighbours.shape, jnp.int32),
             pltpu.VMEM(extrapolator.shape, jnp.float32),
             pltpu.VMEM((2, points, 2 * points), jnp.float32),
-            pltpu.SMEM((10 * tiles,), jnp.int32),
+            pltpu.SMEM((10,), jnp.int32),
             pltpu.SemaphoreType.DMA((1,)),
             pltpu.SemaphoreType.DMA((tiles,)),
         ],
@@ -358,8 +357,7 @@
         for copy in copies:
             copy.start()
         clear_ends(high_ref, low_ref, points)
-        for copy in copies:
-            copy.wait()
+        copies[0].wait()
         half = tiles // 2
         results = [
             (half, pltpu.make_async_copy(made.at[:, :half], out_ref.at[:, :half], stores.at[0])),
@@ -368,6 +366,8 @@
         for t in range(tiles):
             rows = slice(t * points, (t + 1) * points)
             convert((held[0, rows], held[1, rows]), high_ref, low_ref, t)
+        for copy in copies[1:]:
+            copy.wait()
         for t in range(tiles):
             four = product(blocks_ref[t, 1], high_ref, low_ref, t, points)
             real, imaginary = complex_parts(four, points, shots)

time: 38.5 us -> 38.5 us (level)
  transfers between devices with their start and end apart: 7 -> 7, of which waited for: 3 -> 3; matrix products, arithmetic and copies ran while one was open for 0% -> 0% of each run, Pallas kernels for 19% -> 18%
where the time goes in v6:
time: 38.5 us; the launch traced here: 37.8 us
  waiting for transfers between devices  13.6 us (35%)
  starting transfers between devices  12.9 us (34%)
  Pallas kernels  11.2 us (29%)
    ppermute x7, waiting for transfers between devices, send(): return lax.ppermute(value, 'depth', route)  13.6 us
    ppermute x7, starting transfers between devices, send(): return lax.ppermute(value, 'depth', route)  12.9 us
    pallas_call x1, Pallas kernels, arrange(): pl.pallas_call(arrange_kernel, in_specs=[SMEM, HBM, HBM], out_specs=VMEM,...  2.99 us
    pallas_call x2, Pallas kernels, near_sum(): pl.pallas_call(functools.partial(near_kernel, before is None, sends), in_...  2.42 us
    pallas_call x2, Pallas kernels, own_sum(): pl.pallas_call(functools.partial(own_kernel, came is None), in_specs=[SME...  2.08 us
    pallas_call x1, Pallas kernels, first_field(): pl.pallas_call(functools.partial(first_kernel, packs), in_specs=[HBM, HBM...  2.03 us
    pallas_call x2, Pallas kernels, far_sum(): pl.pallas_call(functools.partial(far_kernel, adds), in_specs=[SMEM, VMEM]...  1.65 us
  transfers between devices with their start and end apart: 7, of which 3 were waited for; matrix products, arithmetic and copies ran while one was open for 0% of the time, Pallas kernels for 18%

profile of v6, /device:TPU:24, one launch (start us, length us, event | category | flops | bytes accessed | tf_op | source)
XLA Modules:
  0.0 37.8 jit_solution(5859390230912622039)
XLA Ops:
  0.0 2.0 %shard_map.46 = (f32[2,512,128]{2,1,0:T(8,128)}, f32[2,64,128]{2,1,0:T(8,128)S(1)}) custom-call(f32[2,8,64,128]{3,2,1,0:T(8,128)} %bitcast.5, f32[2,8,64]{2,1,0:T(8,128)} %transmit_ref.5), custom_call_target="tpu_custom_call" | custom-call | flops 500000000 | bytes 4000000 | tf_op jit(solution)/shard_map/pallas_call | solution.py:226
  2.0 1.5 %collective-permute-start.3 = (f32[2,512,128]{2,1,0:T(8,128)}, f32[2,512,128]{2,1,0:T(8,128)}, u32[]{:S(2)}, u32[]{:S(2)}) collective-permute-start(f32[2,512,128]{2,1,0:T(8,128)} %get-tuple-element.17), channel_id=1, source_target_pairs={{1,3},{3,1},{5,7},{7,5},{9,11},{11,9},{13,15},{15,13},{17,19},{19,... | collective-permute-start | bytes 1572872 | tf_op jit(solution)/shard_map/ppermute | solution.py:424
  3.5 1.5 %collective-permute-start = (f32[2,512,128]{2,1,0:T(8,128)}, f32[2,512,128]{2,1,0:T(8,128)}, u32[]{:S(2)}, u32[]{:S(2)}) collective-permute-start(f32[2,512,128]{2,1,0:T(8,128)} %get-tuple-element.17), channel_id=1, source_target_pairs={{3,5},{5,3},{7,9},{9,7},{11,13},{13,11},{19,21},{21,19},{23,25},{2... | collective-permute-start | bytes 1572872 | tf_op jit(solution)/shard_map/ppermute | solution.py:424
  5.0 3.0 %shard_map.47.blocks_ref = bf16[8,3,256,192]{3,2,1,0:T(8,128)(2,1)S(1)} custom-call(s32[1]{0:T(128)} %bitcast.1.strip_ref, s32[8,9]{1,0:T(8,128)} %neighbours_ref.1, f32[8,2,64,576]{3,2,1,0:T(8,128)} %block_ref), custom_call_target="tpu_custom_call" | custom-call | flops 4000000 | bytes 6000000 | tf_op jit(solution)/shard_map/pallas_call | solution.py:72
  8.0 4.8 %collective-permute-start.2 = (f32[2,8,64,128]{3,2,1,0:T(8,128)}, f32[2,8,64,128]{3,2,1,0:T(8,128)}, u32[]{:S(2)}, u32[]{:S(2)}) collective-permute-start(f32[2,8,64,128]{3,2,1,0:T(8,128)} %bitcast.6), channel_id=1, source_target_pairs={{0,1},{2,3},{4,5},{6,7},{8,9},{10,11},{12,13},{14,15},{16,17},{18,... | collective-permute-start | bytes 1572872 | tf_op jit(solution)/shard_map/ppermute | solution.py:424
  12.8 1.3 %collective-permute-start.1 = (f32[2,64,128]{2,1,0:T(8,128)S(1)}, f32[2,64,128]{2,1,0:T(8,128)S(1)}, u32[]{:S(2)}, u32[]{:S(2)}) collective-permute-start(f32[2,64,128]{2,1,0:T(8,128)S(1)} %get-tuple-element.19), channel_id=1, source_target_pairs={{0,1},{2,3},{4,5},{6,7},{8,9},{10,11},{12,13},{14,15},{16,17},{18,... | collective-permute-start | bytes 196616 | tf_op jit(solution)/shard_map/ppermute | solution.py:424
  14.1 0.0 collective-permute-done.refs_1_
  14.2 0.8 %collective-permute-done.1.refs_0_ = f32[2,64,128]{2,1,0:T(8,128)S(1)} collective-permute-done((f32[2,64,128]{2,1,0:T(8,128)S(1)}, f32[2,64,128]{2,1,0:T(8,128)S(1)}, u32[]{:S(2)}, u32[]{:S(2)}) %collective-permute-start.1) | collective-permute-done | bytes 65568 | tf_op jit(solution)/shard_map/ppermute | solution.py:424
  15.0 0.0 collective-permute-done.3.refs_2_
  15.0 0.0 collective-permute-done.2.refs_1_
  15.0 0.1 shard_map.50
  15.0 1.3 %collective-permute-start.5 = (f32[2,512,128]{2,1,0:T(8,128)}, f32[2,512,128]{2,1,0:T(8,128)}, u32[]{:S(2)}, u32[]{:S(2)}) collective-permute-start(f32[2,512,128]{2,1,0:T(8,128)} %get-tuple-element.22), channel_id=1, source_target_pairs={{3,4},{5,2},{7,8},{9,6},{11,12},{13,10},{19,20},{21,18},{23,24},{2... | collective-permute-start | bytes 1572872 | tf_op jit(solution)/shard_map/ppermute | solution.py:424
  16.3 1.3 %collective-permute-start.4 = (f32[2,8,64,128]{3,2,1,0:T(8,128)}, f32[2,8,64,128]{3,2,1,0:T(8,128)}, u32[]{:S(2)}, u32[]{:S(2)}) collective-permute-start(f32[2,8,64,128]{3,2,1,0:T(8,128)} %get-tuple-element.21.refs_0_), channel_id=1, source_target_pairs={{1,0},{3,2},{5,4},{7,6},{9,8},{11,10},{13,12},{15,14},{17,16},{19,... | collective-permute-start | bytes 1572872 | tf_op jit(solution)/shard_map/ppermute | solution.py:424
  17.6 1.3 %collective-permute-start.6 = (f32[2,512,128]{2,1,0:T(8,128)}, f32[2,512,128]{2,1,0:T(8,128)}, u32[]{:S(2)}, u32[]{:S(2)}) collective-permute-start(f32[2,512,128]{2,1,0:T(8,128)} %get-tuple-element.22), channel_id=1, source_target_pairs={{1,2},{3,0},{5,6},{7,4},{9,10},{11,8},{13,14},{15,12},{17,18},{19,... | collective-permute-start | bytes 1572872 | tf_op jit(solution)/shard_map/ppermute | solution.py:424
  18.9 11.0 %collective-permute-done.5.refs_0_ = f32[2,512,128]{2,1,0:T(8,128)} collective-permute-done((f32[2,512,128]{2,1,0:T(8,128)}, f32[2,512,128]{2,1,0:T(8,128)}, u32[]{:S(2)}, u32[]{:S(2)}) %collective-permute-start.5) | collective-permute-done | bytes 524320 | tf_op jit(solution)/shard_map/ppermute | solution.py:424
  29.9 1.6 %shard_map.51.refs_1_ = f32[2,8,64,128]{3,2,1,0:T(8,128)S(1)} custom-call(s32[1]{0:T(128)} %bitcast.active_ref, bf16[8,3,256,192]{3,2,1,0:T(8,128)(2,1)S(1)} %shard_map.47.blocks_ref, f32[2,512,128]{2,1,0:T(8,128)} %collective-permute-done.5.refs_0_), custom_call_target="tpu_custom_call" | custom-call | flops 1000 | bytes 1000 | tf_op jit(solution)/shard_map/pallas_call | solution.py:327
  31.6 0.0 collective-permute-done.4.refs_0_
  31.6 2.0 %shard_map.52.partial_ref = f32[2,8,64,128]{3,2,1,0:T(8,128)S(1)} custom-call(s32[1]{0:T(128)} %bitcast.active_ref, bf16[8,3,256,192]{3,2,1,0:T(8,128)(2,1)S(1)} %shard_map.47.blocks_ref, f32[2,8,64]{2,1,0:T(8,128)} %transmit_ref.5, f32[2,8,64,128]{3,2,1,0:T(8,128)} %bitcast.8, f32[2,8,64,128]{3,2,1,0:T(8,128)} %collective-permute-done.4.refs_0_, ...), custom_call_target="tpu_custom_call" | custom-call | flops 1000 | bytes 1000 | tf_op jit(solution)/shard_map/pallas_call | solution.py:287
  33.6 1.8 %collective-permute-done.6.refs_1_ = f32[2,512,128]{2,1,0:T(8,128)} collective-permute-done((f32[2,512,128]{2,1,0:T(8,128)}, f32[2,512,128]{2,1,0:T(8,128)}, u32[]{:S(2)}, u32[]{:S(2)}) %collective-permute-start.6) | collective-permute-done | bytes 524320 | tf_op jit(solution)/shard_map/ppermute | solution.py:424
  35.5 2.4 %shard_map.53 = f32[2,8,64,128]{3,2,1,0:T(8,128)} custom-call(s32[1]{0:T(128)} %bitcast.active_ref, bf16[8,3,256,192]{3,2,1,0:T(8,128)(2,1)S(1)} %shard_map.47.blocks_ref, f32[2,8,64,128]{3,2,1,0:T(8,128)S(1)} %shard_map.52.partial_ref, f32[2,8,64,128]{3,2,1,0:T(8,128)} %get-tuple-element.21.refs_0_, ...), custom_call_target="tpu_custom_call", output_to_operand_aliasing={{}: (3, {})} | custom-call | flops 1000000000 | bytes 4000000 | tf_op jit(solution)/shard_map/pallas_call | solution.py:412
  (2 shorter events, 0.1 us)
Async XLA Ops:
  2.0 12.9 %collective-permute-start.3 = (f32[2,512,128]{2,1,0:T(8,128)}, f32[2,512,128]{2,1,0:T(8,128)}, u32[]{:S(2)}, u32[]{:S(2)}) collective-permute-start(f32[2,512,128]{2,1,0:T(8,128)} %get-tuple-element.17), channel_id=1, source_target_pairs={{1,3},{3,1},{5,7},{7,5},{9,11},{11,9},{13,15},{15,13},{17,19},{19,... | collective-permute-start | bytes 1572872 | tf_op jit(solution)/shard_map/ppermute | solution.py:424
  3.5 10.6 %collective-permute-start = (f32[2,512,128]{2,1,0:T(8,128)}, f32[2,512,128]{2,1,0:T(8,128)}, u32[]{:S(2)}, u32[]{:S(2)}) collective-permute-start(f32[2,512,128]{2,1,0:T(8,128)} %get-tuple-element.17), channel_id=1, source_target_pairs={{3,5},{5,3},{7,9},{9,7},{11,13},{13,11},{19,21},{21,19},{23,25},{2... | collective-permute-start | bytes 1572872 | tf_op jit(solution)/shard_map/ppermute | solution.py:424
  8.0 7.0 %collective-permute-start.2 = (f32[2,8,64,128]{3,2,1,0:T(8,128)}, f32[2,8,64,128]{3,2,1,0:T(8,128)}, u32[]{:S(2)}, u32[]{:S(2)}) collective-permute-start(f32[2,8,64,128]{3,2,1,0:T(8,128)} %bitcast.6), channel_id=1, source_target_pairs={{0,1},{2,3},{4,5},{6,7},{8,9},{10,11},{12,13},{14,15},{16,17},{18,... | collective-permute-start | bytes 1572872 | tf_op jit(solution)/shard_map/ppermute | solution.py:424
  12.8 2.2 %collective-permute-start.1 = (f32[2,64,128]{2,1,0:T(8,128)S(1)}, f32[2,64,128]{2,1,0:T(8,128)S(1)}, u32[]{:S(2)}, u32[]{:S(2)}) collective-permute-start(f32[2,64,128]{2,1,0:T(8,128)S(1)} %get-tuple-element.19), channel_id=1, source_target_pairs={{0,1},{2,3},{4,5},{6,7},{8,9},{10,11},{12,13},{14,15},{16,17},{18,... | collective-permute-start | bytes 196616 | tf_op jit(solution)/shard_map/ppermute | solution.py:424
  15.0 14.9 %collective-permute-start.5 = (f32[2,512,128]{2,1,0:T(8,128)}, f32[2,512,128]{2,1,0:T(8,128)}, u32[]{:S(2)}, u32[]{:S(2)}) collective-permute-start(f32[2,512,128]{2,1,0:T(8,128)} %get-tuple-element.22), channel_id=1, source_target_pairs={{3,4},{5,2},{7,8},{9,6},{11,12},{13,10},{19,20},{21,18},{23,24},{2... | collective-permute-start | bytes 1572872 | tf_op jit(solution)/shard_map/ppermute | solution.py:424
  16.3 15.2 %collective-permute-start.4 = (f32[2,8,64,128]{3,2,1,0:T(8,128)}, f32[2,8,64,128]{3,2,1,0:T(8,128)}, u32[]{:S(2)}, u32[]{:S(2)}) collective-permute-start(f32[2,8,64,128]{3,2,1,0:T(8,128)} %get-tuple-element.21.refs_0_), channel_id=1, source_target_pairs={{1,0},{3,2},{5,4},{7,6},{9,8},{11,10},{13,12},{15,14},{17,16},{19,... | collective-permute-start | bytes 1572872 | tf_op jit(solution)/shard_map/ppermute | solution.py:424
  17.6 17.8 %collective-permute-start.6 = (f32[2,512,128]{2,1,0:T(8,128)}, f32[2,512,128]{2,1,0:T(8,128)}, u32[]{:S(2)}, u32[]{:S(2)}) collective-permute-start(f32[2,512,128]{2,1,0:T(8,128)} %get-tuple-element.22), channel_id=1, source_target_pairs={{1,2},{3,0},{5,6},{7,4},{9,10},{11,8},{13,14},{15,12},{17,18},{19,... | collective-permute-start | bytes 1572872 | tf_op jit(solution)/shard_map/ppermute | solution.py:424
